TPU v7x, 256 devices: a whole 4x4x8 slice. The times are simulated.
256 devices in a mesh: ctx: 64 (over y, z, core), head: 4 (over x).
Axes of the slice: x: 4, y: 4, z: 8, core: 2. Of those that a mesh axis runs over, the one named last changes fastest.
Arguments:
- queries: bfloat16 [65536, 512], P('ctx', 'head'), may hold values from -18 to 18
- key_states: bfloat16 [65536, 512], P('ctx', 'head'), may hold values from -6 to 6
- value_states: bfloat16 [65536, 512], P('ctx', 'head'), may hold values from -6 to 6
- clip_lengths: int32 [8], replicated, may hold values from 1 to 128, 512 in all
- out_weight: bfloat16 [512, 6144], P(None, 'head'), may hold values from -0.25 to 0.25
Outputs:
- projected: bfloat16 [65536, 6144], P('ctx', 'head')
Inputs may be any that keep to these rules, and one draw needn't show every extreme that they name: clip_lengths[c] counts the 128-token blocks of clip c; the clips lie end to end and fill all 512 blocks; the longest has exactly 128 blocks.
All inputs are finite; a program needn't handle non-finite values.
Results may differ from a plain program's by a relative error of at most 0.015.
Values may be sent and summed in bfloat16 or wider, within the bound.
No kernel may reach another device: no remote copies, remote signals or barrier semaphores. Data moves between devices by JAX's collectives and lax.ppermute only.
A program may use at most 128 MiB of HBM per device.

v0:
```python
import functools
import math

import jax
import jax.numpy as jnp
from jax import lax
from jax.experimental import pallas as pl
from jax.experimental.pallas import tpu as pltpu
from jax.sharding import PartitionSpec as P

HEAD_DIM = 128
BLOCK = 128
FAR = -1e30
START = -1e25
TO_LOG2 = math.log2(math.e) * HEAD_DIM**-0.5
VMEM_LIMIT = 16 * 2**20
KEY_TILE = 256
RING_CHIPS = 8


def vmem_spec():
    return pl.BlockSpec(memory_space=pltpu.VMEM)


def smem_spec():
    return pl.BlockSpec(memory_space=pltpu.SMEM)


def fold_kernel(first, parts, info, key_base, *refs):
    count = len(parts)
    q_refs, kv, refs = refs[:count], refs[count], refs[count + 1 :]
    if first:
        m_out, a_out, v_wide, q_all = refs
        m_in, a_in = m_out, a_out
        m_out[...] = jnp.full(m_out.shape, START, jnp.float32)
        a_out[...] = jnp.zeros(a_out.shape, jnp.float32)
    else:
        m_in, a_in, m_out, a_out, v_wide, q_all = refs
    tok = q_refs[0].shape[0]
    blocks = tok // BLOCK
    k_base = key_base[0]

    def wants(part):
        return (k_base + blocks > info[4 + part * blocks]) & (k_base < info[part] + blocks)

    any_wants = False
    for part, q_ref in zip(parts, q_refs):
        any_wants = any_wants | wants(part)

        @pl.when(wants(part))
        def _(part=part, q_ref=q_ref):
            q_all[part - parts[0]] = q_ref[...]

    @pl.when(any_wants)
    def _():
        v_wide[:, :HEAD_DIM] = kv[1]
        v_wide[:, HEAD_DIM:] = jnp.ones((tok, HEAD_DIM), jnp.bfloat16)

    @pl.loop(parts[0], parts[0] + count)
    def _(part):
        rows = pl.ds(pl.multiple_of(part * tok, tok), tok)
        q_base = info[part]
        begin = [info[4 + part * blocks + i] for i in range(blocks)]

        @pl.when(wants(part))
        def _():
            q = q_all[part - parts[0]]
            m = m_in[rows, :]
            acc = a_in[rows, :]
            for t in range(tok // KEY_TILE):
                keys = slice(t * KEY_TILE, (t + 1) * KEY_TILE)
                s = lax.dot_general(
                    q, kv[0, keys, :], (((1,), (1,)), ((), ())), preferred_element_type=jnp.float32
                )
                columns = []
                for j in range(KEY_TILE // BLOCK):
                    k_blk = k_base + t * (KEY_TILE // BLOCK) + j
                    column = []
                    for i in range(blocks):
                        seen = (k_blk >= begin[i]) & (k_blk <= q_base + i)
                        bias = jnp.where(seen, 0.0, FAR).astype(jnp.float32)
                        column.append(
                            s[i * BLOCK : (i + 1) * BLOCK, j * BLOCK : (j + 1) * BLOCK] + bias
                        )
                    columns.append(jnp.concatenate(column, axis=0))
                s = jnp.concatenate(columns, axis=1)
                new_m = jnp.maximum(m, jnp.max(s, axis=1, keepdims=True) * TO_LOG2)
                factor = jnp.exp2(m - new_m)
                p = jnp.exp2(s * TO_LOG2 - jnp.concatenate([new_m] * (KEY_TILE // HEAD_DIM), axis=1))
                added = jnp.dot(
                    p.astype(jnp.bfloat16), v_wide[keys, :], preferred_element_type=jnp.float32
                )
                acc = acc * jnp.concatenate([factor] * 2, axis=1) + added
                m = new_m
            m_out[rows, :] = m
            a_out[rows, :] = acc


def fold(info, key_base, q_parts, parts, kv, state, weight=46):
    tok = q_parts[0].shape[0]
    first = state is None
    count = len(parts)
    shapes = [
        pltpu.VMEM((4 * tok, HEAD_DIM), jnp.float32),
        pltpu.VMEM((4 * tok, 2 * HEAD_DIM), jnp.float32),
    ]
    return pl.pallas_call(
        functools.partial(fold_kernel, first, parts),
        out_shape=shapes,
        in_specs=[smem_spec()] * 2 + [vmem_spec()] * (count + (1 if first else 3)),
        out_specs=[vmem_spec()] * 2,
        scratch_shapes=[
            pltpu.VMEM((tok, 2 * HEAD_DIM), jnp.bfloat16),
            pltpu.VMEM((count, tok, HEAD_DIM), jnp.bfloat16),
        ],
        input_output_aliases={} if first else {count + 3: 0, count + 4: 1},
        compiler_params=pltpu.CompilerParams(vmem_limit_bytes=VMEM_LIMIT),
        cost_estimate=pl.CostEstimate(
            flops=weight * tok * tok * HEAD_DIM, bytes_accessed=10**6, transcendentals=2 * tok * tok
        ),
        name="fold",
    )(info, key_base, *[q_parts[p] for p in parts], kv, *(() if first else state))


def diagonal():
    row = lax.broadcasted_iota(jnp.int32, (BLOCK, BLOCK), 0)
    return row == lax.broadcasted_iota(jnp.int32, (BLOCK, BLOCK), 1)


def pack(out_ref, out, log_sum):
    tok = out.shape[0]
    blocks = tok // BLOCK
    on = diagonal()
    rows = [
        jnp.sum(jnp.where(on, log_sum[i * BLOCK : (i + 1) * BLOCK, :], 0.0), axis=0, keepdims=True)
        for i in range(blocks)
    ]
    rest = jnp.concatenate(rows, axis=0)
    out_ref[:tok, :] = out.astype(jnp.bfloat16)
    for k in range(3):
        piece = rest.astype(jnp.bfloat16)
        rest = rest - piece.astype(jnp.float32)
        both = jnp.concatenate([piece.astype(jnp.float32), jnp.zeros((blocks, BLOCK), jnp.float32)])
        out_ref[tok + 2 * blocks * k : tok + 2 * blocks * (k + 1), :] = both.astype(jnp.bfloat16)


def unpack(ref, tok):
    blocks = tok // BLOCK
    on = diagonal()
    tail = ref[tok:, :].astype(jnp.float32)
    log_rows = sum(tail[2 * blocks * k : 2 * blocks * k + blocks, :] for k in range(3))
    columns = [
        jnp.sum(jnp.where(on, log_rows[i : i + 1, :], 0.0), axis=1, keepdims=True)
        for i in range(blocks)
    ]
    return ref[:tok, :].astype(jnp.float32), jnp.concatenate(columns, axis=0)


def packed_shape(tok):
    return jax.ShapeDtypeStruct((tok + 6 * (tok // BLOCK), HEAD_DIM), jnp.bfloat16)


def own_part(m_ref, a_ref, rows):
    return m_ref[rows, :], a_ref[rows, :HEAD_DIM], a_ref[rows, HEAD_DIM:]


def pack_state(out_ref, m, num, den):
    some = den > 0.0
    safe = jnp.where(some, den, 1.0)
    pack(out_ref, num / safe, jnp.where(some, m + jnp.log2(safe), START))


def mix(m, num, den, out, log_sum):
    top = jnp.maximum(m, log_sum)
    here = jnp.exp2(m - top)
    there = jnp.exp2(log_sum - top)
    return top, num * here + out * there, den * here + there * (log_sum > 0.5 * START)


def leave_kernel(tok, part, m_ref, a_ref, out_ref):
    pack_state(out_ref, *own_part(m_ref, a_ref, slice(part * tok, (part + 1) * tok)))


def pass_on_kernel(tok, part, m_ref, a_ref, other, out_ref):
    state = own_part(m_ref, a_ref, slice(part * tok, (part + 1) * tok))
    pack_state(out_ref, *mix(*state, *unpack(other, tok)))


def join_kernel(tok, m_ref, a_ref, other, back, out_ref):
    state = mix(*own_part(m_ref, a_ref, slice(0, tok)), *unpack(other, tok))
    _, num, den = mix(*state, *unpack(back, tok))
    out_ref[...] = (num / den).astype(jnp.bfloat16)


def small_call(kernel, name, out_shape, *args):
    return pl.pallas_call(
        kernel,
        out_shape=out_shape,
        in_specs=[vmem_spec()] * len(args),
        out_specs=vmem_spec(),
        compiler_params=pltpu.CompilerParams(vmem_limit_bytes=VMEM_LIMIT),
        name=name,
    )(*args)


def project_kernel(heads, own, left, right, far, weight, out_ref, lhs):
    step = pl.program_id(0)
    h = heads[0]
    count = weight.shape[0] // HEAD_DIM
    width = out_ref.shape[1]

    @pl.when(step == 0)
    def _():
        for by, piece in ((0, own), (count - 1, left), (1, right), (2, far)):
            column = pl.multiple_of(lax.rem(h + by, count) * HEAD_DIM, HEAD_DIM)
            lhs[:, pl.ds(column, HEAD_DIM)] = piece[...]

    columns = pl.ds(pl.multiple_of(step * width, width), width)
    out_ref[...] = jnp.dot(
        lhs[...], weight[:, columns], preferred_element_type=jnp.float32
    ).astype(jnp.bfloat16)


def project(heads, pieces, weight):
    tok = pieces[0].shape[0]
    steps = 3
    width = weight.shape[1] // steps
    return pl.pallas_call(
        project_kernel,
        grid=(steps,),
        out_shape=jax.ShapeDtypeStruct((tok, weight.shape[1]), jnp.bfloat16),
        in_specs=[smem_spec()] + [vmem_spec()] * 5,
        out_specs=pl.BlockSpec((tok, width), lambda i: (0, i)),
        scratch_shapes=[pltpu.VMEM((tok, weight.shape[0]), jnp.bfloat16)],
        compiler_params=pltpu.CompilerParams(vmem_limit_bytes=VMEM_LIMIT),
        name="project",
    )(heads, *pieces, weight)


def shards(queries, key_states, value_states, clip_lengths, out_weight):
    tok = queries.shape[0]
    blocks = tok // BLOCK
    ctx_count = lax.axis_size("ctx")
    head_count = lax.axis_size("head")
    ring = 2 * RING_CHIPS
    me = lax.axis_index("ctx")
    core = me % 2
    first_of_ring = me // ring * ring
    place = (me % ring) // 2
    head = lax.axis_index("head")

    def send(value, target):
        return lax.ppermute(value, "ctx", [(i, target(i)) for i in range(ctx_count)])

    def sibling(i):
        return i ^ 1

    def along(i):
        at = i % ring
        by = 2 if i % 2 == 0 else -2
        return i - at + (at + by) % ring

    def after(value, state):
        value, m = lax.optimization_barrier((value, state[0]))
        return value, (m, state[1])

    def up(i):
        return (i + ring) % ctx_count

    def down(i):
        return (i - ring) % ctx_count

    def turn(value, by):
        pairs = [(i, (i + by) % head_count) for i in range(head_count)]
        return lax.ppermute(value, "head", pairs)

    kv = jnp.stack([key_states, value_states])
    near = send(kv, along)
    cross = send(kv, lambda i: along(sibling(i)))
    next_own = send(queries, down)
    q_sibling = send(queries, sibling)

    upto = jnp.arange(clip_lengths.shape[0])
    ends = jnp.sum(jnp.where(upto[None, :] <= upto[:, None], clip_lengths[None, :], 0), axis=1)
    owners = jnp.stack([me, me ^ 1, (me + ring) % ctx_count, ((me + ring) % ctx_count) ^ 1])
    bases = owners * blocks
    q_blocks = bases[:, None] + jnp.arange(blocks, dtype=jnp.int32)[None, :]
    begin = jnp.max(
        jnp.where(ends[None, None, :] <= q_blocks[:, :, None], ends[None, None, :], 0), axis=-1
    )
    info = jnp.concatenate([bases, begin.reshape(-1)]).astype(jnp.int32)

    def base_of(step, of_core):
        chip = (place + jnp.where(core == 0, -step, step)) % RING_CHIPS
        return ((first_of_ring + 2 * chip + of_core) * blocks).reshape(1).astype(jnp.int32)

    order = []
    for step in range(1, RING_CHIPS // 2 + 1):
        order += [(step, core), (step, 1 - core)]
    order = order[:-1]
    arrived = [near, cross]
    everyone = (0, 1, 2, 3)
    own_base = base_of(0, core)
    state = fold(info, own_base, (queries,), (0,), kv, None, 4)
    state = fold(info, own_base, (queries, q_sibling), (1,), kv, state, 4)
    q_parts = (queries, q_sibling, next_own, send(queries, lambda i: sibling(down(i))))
    for n, (step, of_core) in enumerate(order):
        value = arrived[n]
        if n + 2 < len(order):
            value, state = after(value, state)
            arrived.append(send(value, along))
        if n == len(order) - 1:
            state = fold(info, own_base, q_parts, (2, 3), kv, state)
        state = fold(
            info, base_of(step, of_core), q_parts, everyone, value, state, 46 if n else 8
        )

    packed = packed_shape(tok)
    leave = functools.partial(leave_kernel, tok)
    next_there = send(small_call(functools.partial(leave, 3), "leave_next", packed, *state), sibling)
    own_there = send(small_call(functools.partial(leave, 1), "leave_own", packed, *state), sibling)
    passed = small_call(
        functools.partial(pass_on_kernel, tok, 2), "pass_on", packed, *state, next_there
    )
    back = send(passed, up)
    attended = small_call(
        functools.partial(join_kernel, tok),
        "join",
        jax.ShapeDtypeStruct((tok, HEAD_DIM), jnp.bfloat16),
        *state,
        own_there,
        back,
    )
    pieces = (attended, turn(attended, 1), turn(attended, -1), turn(attended, 2))
    return project(head.reshape(1).astype(jnp.int32), pieces, out_weight)


def solution(mesh):
    placed = (P("ctx", "head"), P("ctx", "head"), P("ctx", "head"), P(), P(None, "head"))
    return jax.shard_map(
        shards, mesh=mesh, in_specs=placed, out_specs=P("ctx", "head"), check_vma=False
    )
```

profile of v0, /device:TPU:1, one launch (start us, length us, event | category | flops | bytes accessed | tf_op | source)
XLA Modules:
  0.0 90.7 jit_solution(6301662825676599372)
XLA Ops:
  0.0 4.1 %collective-permute-start.2 = (bf16[1024,128]{1,0:T(8,128)(2,1)}, bf16[1024,128]{1,0:T(8,128)(2,1)S(1)}, u32[]{:S(2)}, u32[]{:S(2)}) collective-permute-start(bf16[1024,128]{1,0:T(8,128)(2,1)} %refs_0_.15), channel_id=1, source_target_pairs={{0,196},{4,192},{8,204},{12,200},{16,212},{20,208},{24,220},{28,21... | collective-permute-start | bytes 786440 | tf_op jit(solution)/shard_map/ppermute | solution.py:253
  4.1 0.5 collective-permute-start.1
  4.6 0.1 collective-permute-start
  4.7 1.1 %pad_maximum_fusion.refs_1_.refs_2_ = bf16[2,1024,128]{2,1,0:T(8,128)(2,1)S(1)} fusion(bf16[1,1024,128]{2,1,0:T(8,128)(2,1)} %bitcast.15, bf16[1,1024,128]{2,1,0:T(8,128)(2,1)} %bitcast.16), kind=kLoop, calls=%fused_computation | loop fusion | flops 262144 | bytes 1048576 | tf_op jit(solution)/shard_map/stack | solution.py:277
  5.8 2.0 %collective-permute-start.5 = (bf16[2,1024,128]{2,1,0:T(8,128)(2,1)S(1)}, bf16[2,1024,128]{2,1,0:T(8,128)(2,1)S(1)}, u32[]{:S(2)}, u32[]{:S(2)}) collective-permute-start(bf16[2,1024,128]{2,1,0:T(8,128)(2,1)S(1)} %pad_maximum_fusion.refs_1_.refs_2_), channel_id=1, source_target_pairs={{0,60},{4,8},{8,4},{12,16},{16,12},{20,24},{24,20},{28,32},{32,28}... | collective-permute-start | bytes 1572872 | tf_op jit(solution)/shard_map/ppermute | solution.py:253
  7.8 3.7 %collective-permute-start.3 = (bf16[2,1024,128]{2,1,0:T(8,128)(2,1)S(1)}, bf16[2,1024,128]{2,1,0:T(8,128)(2,1)S(1)}, u32[]{:S(2)}, u32[]{:S(2)}) collective-permute-start(bf16[2,1024,128]{2,1,0:T(8,128)(2,1)S(1)} %pad_maximum_fusion.refs_1_.refs_2_), channel_id=1, source_target_pairs={{0,8},{4,60},{8,16},{12,4},{16,24},{20,12},{24,32},{28,20},{32,40}... | collective-permute-start | bytes 1572872 | tf_op jit(solution)/shard_map/ppermute | solution.py:253
  11.5 0.1 add_multiply_fusion
  11.7 0.8 select_reduce_fusion.1
  12.5 0.2 select_reduce_fusion
  12.8 0.1 reshape.86
  13.0 0.9 %copy-done.1 = bf16[1024,128]{1,0:T(8,128)(2,1)S(1)} copy-done((bf16[1024,128]{1,0:T(8,128)(2,1)S(1)}, bf16[1024,128]{1,0:T(8,128)(2,1)}, u32[]{:S(2)}) %copy-start.1) | copy-done | bytes 262168
  13.9 2.8 %fold.10 = (f32[4096,128]{1,0:T(8,128)S(1)}, f32[4096,256]{1,0:T(8,128)S(1)}) custom-call(s32[36]{0:T(128)S(1)} %pad_add_fusion.info, s32[1]{0:T(128)} %bitcast.8.key_base, bf16[1024,128]{1,0:T(8,128)(2,1)S(1)} %copy-done.1, bf16[2,1024,128]{2,1,0:T(8,128)(2,1)S(1)} %pad_maximum_fusion.refs_1_.refs_2_), custom_call_target="tpu_custom_call" | custom-call | flops 536870912 | bytes 1000000 | tf_op jit(solution)/shard_map/fold/pallas_call | solution.py:107
  16.8 0.6 fold.11
  17.4 5.5 %collective-permute-done.3.refs_4_ = bf16[2,1024,128]{2,1,0:T(8,128)(2,1)S(1)} collective-permute-done((bf16[2,1024,128]{2,1,0:T(8,128)(2,1)S(1)}, bf16[2,1024,128]{2,1,0:T(8,128)(2,1)S(1)}, u32[]{:S(2)}, u32[]{:S(2)}) %collective-permute-start.3) | collective-permute-done | bytes 524320 | tf_op jit(solution)/shard_map/ppermute | solution.py:253
  22.9 3.1 %collective-permute-start.4 = (bf16[2,1024,128]{2,1,0:T(8,128)(2,1)S(1)}, bf16[2,1024,128]{2,1,0:T(8,128)(2,1)S(1)}, u32[]{:S(2)}, u32[]{:S(2)}) collective-permute-start(bf16[2,1024,128]{2,1,0:T(8,128)(2,1)S(1)} %collective-permute-done.3.refs_4_), channel_id=1, source_target_pairs={{0,8},{4,60},{8,16},{12,4},{16,24},{20,12},{24,32},{28,20},{32,40}... | collective-permute-start | bytes 1572872 | tf_op jit(solution)/shard_map/ppermute | solution.py:253
  26.0 0.7 fold.12
  26.7 0.5 collective-permute-start.7
  27.2 0.8 fold.13
  28.0 4.1 %collective-permute-done.4.refs_4_ = bf16[2,1024,128]{2,1,0:T(8,128)(2,1)S(1)} collective-permute-done((bf16[2,1024,128]{2,1,0:T(8,128)(2,1)S(1)}, bf16[2,1024,128]{2,1,0:T(8,128)(2,1)S(1)}, u32[]{:S(2)}, u32[]{:S(2)}) %collective-permute-start.4) | collective-permute-done | bytes 524320 | tf_op jit(solution)/shard_map/ppermute | solution.py:253
  32.1 3.1 %collective-permute-start.6 = (bf16[2,1024,128]{2,1,0:T(8,128)(2,1)S(1)}, bf16[2,1024,128]{2,1,0:T(8,128)(2,1)S(1)}, u32[]{:S(2)}, u32[]{:S(2)}) collective-permute-start(bf16[2,1024,128]{2,1,0:T(8,128)(2,1)S(1)} %collective-permute-done.4.refs_4_), channel_id=1, source_target_pairs={{0,8},{4,60},{8,16},{12,4},{16,24},{20,12},{24,32},{28,20},{32,40}... | collective-permute-start | bytes 1572872 | tf_op jit(solution)/shard_map/ppermute | solution.py:253
  35.2 0.7 fold.14
  35.9 1.8 %collective-permute-done.7.refs_4_ = bf16[2,1024,128]{2,1,0:T(8,128)(2,1)S(1)} collective-permute-done((bf16[2,1024,128]{2,1,0:T(8,128)(2,1)S(1)}, bf16[2,1024,128]{2,1,0:T(8,128)(2,1)S(1)}, u32[]{:S(2)}, u32[]{:S(2)}) %collective-permute-start.7) | collective-permute-done | bytes 524320 | tf_op jit(solution)/shard_map/ppermute | solution.py:253
  37.7 3.1 %collective-permute-start.9 = (bf16[2,1024,128]{2,1,0:T(8,128)(2,1)S(1)}, bf16[2,1024,128]{2,1,0:T(8,128)(2,1)S(1)}, u32[]{:S(2)}, u32[]{:S(2)}) collective-permute-start(bf16[2,1024,128]{2,1,0:T(8,128)(2,1)S(1)} %collective-permute-done.7.refs_4_), channel_id=1, source_target_pairs={{0,8},{4,60},{8,16},{12,4},{16,24},{20,12},{24,32},{28,20},{32,40}... | collective-permute-start | bytes 1572872 | tf_op jit(solution)/shard_map/ppermute | solution.py:253
  40.8 0.7 fold.15
  41.5 1.8 %collective-permute-done.6.refs_4_ = bf16[2,1024,128]{2,1,0:T(8,128)(2,1)S(1)} collective-permute-done((bf16[2,1024,128]{2,1,0:T(8,128)(2,1)S(1)}, bf16[2,1024,128]{2,1,0:T(8,128)(2,1)S(1)}, u32[]{:S(2)}, u32[]{:S(2)}) %collective-permute-start.6) | collective-permute-done | bytes 524320 | tf_op jit(solution)/shard_map/ppermute | solution.py:253
  43.3 3.1 %collective-permute-start.8 = (bf16[2,1024,128]{2,1,0:T(8,128)(2,1)S(1)}, bf16[2,1024,128]{2,1,0:T(8,128)(2,1)S(1)}, u32[]{:S(2)}, u32[]{:S(2)}) collective-permute-start(bf16[2,1024,128]{2,1,0:T(8,128)(2,1)S(1)} %collective-permute-done.6.refs_4_), channel_id=1, source_target_pairs={{0,8},{4,60},{8,16},{12,4},{16,24},{20,12},{24,32},{28,20},{32,40}... | collective-permute-start | bytes 1572872 | tf_op jit(solution)/shard_map/ppermute | solution.py:253
  46.5 0.7 fold.16
  47.1 1.8 %collective-permute-done.9.refs_4_ = bf16[2,1024,128]{2,1,0:T(8,128)(2,1)S(1)} collective-permute-done((bf16[2,1024,128]{2,1,0:T(8,128)(2,1)S(1)}, bf16[2,1024,128]{2,1,0:T(8,128)(2,1)S(1)}, u32[]{:S(2)}, u32[]{:S(2)}) %collective-permute-start.9) | collective-permute-done | bytes 524320 | tf_op jit(solution)/shard_map/ppermute | solution.py:253
  49.0 0.7 fold.17
  49.6 0.8 fold.18
  50.5 4.1 %collective-permute-done.8.refs_4_ = bf16[2,1024,128]{2,1,0:T(8,128)(2,1)S(1)} collective-permute-done((bf16[2,1024,128]{2,1,0:T(8,128)(2,1)S(1)}, bf16[2,1024,128]{2,1,0:T(8,128)(2,1)S(1)}, u32[]{:S(2)}, u32[]{:S(2)}) %collective-permute-start.8) | collective-permute-done | bytes 524320 | tf_op jit(solution)/shard_map/ppermute | solution.py:253
  54.6 0.7 fold.19
  55.3 0.2 leave_next.1
  55.5 5.0 %collective-permute-start.11 = (bf16[1072,128]{1,0:T(8,128)(2,1)S(1)}, bf16[1072,128]{1,0:T(8,128)(2,1)S(1)}, u32[]{:S(2)}, u32[]{:S(2)}) collective-permute-start(bf16[1072,128]{1,0:T(8,128)(2,1)S(1)} %leave_next.1), channel_id=1, source_target_pairs={{0,4},{4,0},{8,12},{12,8},{16,20},{20,16},{24,28},{28,24},{32,36},... | collective-permute-start | bytes 823304 | tf_op jit(solution)/shard_map/ppermute | solution.py:253
  60.4 0.2 leave_own.1
  60.6 0.1 collective-permute-start.10
  60.7 0.9 collective-permute-done.11.other
  61.6 0.7 pass_on.1
  62.3 0.1 collective-permute-start.12
  62.4 9.0 %collective-permute-done.12.back = bf16[1072,128]{1,0:T(8,128)(2,1)S(1)} collective-permute-done((bf16[1072,128]{1,0:T(8,128)(2,1)S(1)}, bf16[1072,128]{1,0:T(8,128)(2,1)S(1)}, u32[]{:S(2)}, u32[]{:S(2)}) %collective-permute-start.12) | collective-permute-done | bytes 274464 | tf_op jit(solution)/shard_map/ppermute | solution.py:253
  71.4 1.0 %join.1.own = bf16[1024,128]{1,0:T(8,128)(2,1)S(1)} custom-call(f32[4096,128]{1,0:T(8,128)S(1)} %get-tuple-element.63.m_ref, f32[4096,256]{1,0:T(8,128)S(1)} %get-tuple-element.64.a_ref, bf16[1072,128]{1,0:T(8,128)(2,1)S(1)} %collective-permute-done.10.other, bf16[1072,128]{1,0:T(8,128)(2,1)S(1)} %collective-permute-done.12.back), custom_call_target="tpu_custom_call" | custom-call | tf_op jit(solution)/shard_map/join/pallas_call | solution.py:196
  72.4 2.8 %collective-permute-start.15 = (bf16[1024,128]{1,0:T(8,128)(2,1)S(1)}, bf16[1024,128]{1,0:T(8,128)(2,1)S(1)}, u32[]{:S(2)}, u32[]{:S(2)}) collective-permute-start(bf16[1024,128]{1,0:T(8,128)(2,1)S(1)} %join.1.own), channel_id=1, source_target_pairs={{0,2},{1,3},{2,0},{3,1},{4,6},{5,7},{6,4},{7,5},{8,10},{9,11},{10,... | collective-permute-start | bytes 786440 | tf_op jit(solution)/shard_map/ppermute | solution.py:275
  75.2 0.9 collective-permute-start.14
  76.1 0.6 collective-permute-start.13
  76.7 3.9 %collective-permute-done.15.far = bf16[1024,128]{1,0:T(8,128)(2,1)S(1)} collective-permute-done((bf16[1024,128]{1,0:T(8,128)(2,1)S(1)}, bf16[1024,128]{1,0:T(8,128)(2,1)S(1)}, u32[]{:S(2)}, u32[]{:S(2)}) %collective-permute-start.15) | collective-permute-done | bytes 262176 | tf_op jit(solution)/shard_map/ppermute | solution.py:275
  80.6 6.3 %collective-permute-done.14.right = bf16[1024,128]{1,0:T(8,128)(2,1)S(1)} collective-permute-done((bf16[1024,128]{1,0:T(8,128)(2,1)S(1)}, bf16[1024,128]{1,0:T(8,128)(2,1)S(1)}, u32[]{:S(2)}, u32[]{:S(2)}) %collective-permute-start.14) | collective-permute-done | bytes 262176 | tf_op jit(solution)/shard_map/ppermute | solution.py:275
  86.9 0.1 collective-permute-done.13.left
  87.0 3.6 %project.1 = bf16[1024,1536]{1,0:T(8,128)(2,1)} custom-call(s32[1]{0:T(128)} %bitcast.heads, bf16[1024,128]{1,0:T(8,128)(2,1)S(1)} %join.1.own, bf16[1024,128]{1,0:T(8,128)(2,1)S(1)} %collective-permute-done.13.left, bf16[1024,128]{1,0:T(8,128)(2,1)S(1)} %collective-permute-done.14.right, bf16[1024,128]{1,0:T(8,128)(2,1)S(1)} %collective-permute-done.15.far, ...), custom_call_target="tpu_custom_call" | custom-call | tf_op jit(solution)/shard_map/project/pallas_call | solution.py:228
  (10 shorter events, 0.2 us)
Async XLA Ops:
  0.0 26.0 %collective-permute-start.2 = (bf16[1024,128]{1,0:T(8,128)(2,1)}, bf16[1024,128]{1,0:T(8,128)(2,1)S(1)}, u32[]{:S(2)}, u32[]{:S(2)}) collective-permute-start(bf16[1024,128]{1,0:T(8,128)(2,1)} %refs_0_.15), channel_id=1, source_target_pairs={{0,196},{4,192},{8,204},{12,200},{16,212},{20,208},{24,220},{28,21... | collective-permute-start | bytes 786440 | tf_op jit(solution)/shard_map/ppermute | solution.py:253
  4.1 21.9 %collective-permute-start.1 = (bf16[1024,128]{1,0:T(8,128)(2,1)}, bf16[1024,128]{1,0:T(8,128)(2,1)S(1)}, u32[]{:S(2)}, u32[]{:S(2)}) collective-permute-start(bf16[1024,128]{1,0:T(8,128)(2,1)} %refs_0_.15), channel_id=1, source_target_pairs={{0,192},{4,196},{8,200},{12,204},{16,208},{20,212},{24,216},{28,22... | collective-permute-start | bytes 786440 | tf_op jit(solution)/shard_map/ppermute | solution.py:253
  4.6 12.2 %collective-permute-start = (bf16[1024,128]{1,0:T(8,128)(2,1)}, bf16[1024,128]{1,0:T(8,128)(2,1)S(1)}, u32[]{:S(2)}, u32[]{:S(2)}) collective-permute-start(bf16[1024,128]{1,0:T(8,128)(2,1)} %refs_0_.15), channel_id=1, source_target_pairs={{0,4},{4,0},{8,12},{12,8},{16,20},{20,16},{24,28},{28,24},{32,36},... | collective-permute-start | bytes 786440 | tf_op jit(solution)/shard_map/ppermute | solution.py:253
  5.8 20.9 %collective-permute-start.5 = (bf16[2,1024,128]{2,1,0:T(8,128)(2,1)S(1)}, bf16[2,1024,128]{2,1,0:T(8,128)(2,1)S(1)}, u32[]{:S(2)}, u32[]{:S(2)}) collective-permute-start(bf16[2,1024,128]{2,1,0:T(8,128)(2,1)S(1)} %pad_maximum_fusion.refs_1_.refs_2_), channel_id=1, source_target_pairs={{0,60},{4,8},{8,4},{12,16},{16,12},{20,24},{24,20},{28,32},{32,28}... | collective-permute-start | bytes 1572872 | tf_op jit(solution)/shard_map/ppermute | solution.py:253
  7.8 15.1 %collective-permute-start.3 = (bf16[2,1024,128]{2,1,0:T(8,128)(2,1)S(1)}, bf16[2,1024,128]{2,1,0:T(8,128)(2,1)S(1)}, u32[]{:S(2)}, u32[]{:S(2)}) collective-permute-start(bf16[2,1024,128]{2,1,0:T(8,128)(2,1)S(1)} %pad_maximum_fusion.refs_1_.refs_2_), channel_id=1, source_target_pairs={{0,8},{4,60},{8,16},{12,4},{16,24},{20,12},{24,32},{28,20},{32,40}... | collective-permute-start | bytes 1572872 | tf_op jit(solution)/shard_map/ppermute | solution.py:253
  13.0 1.0 %copy-start.1 = (bf16[1024,128]{1,0:T(8,128)(2,1)S(1)}, bf16[1024,128]{1,0:T(8,128)(2,1)}, u32[]{:S(2)}) copy-start(bf16[1024,128]{1,0:T(8,128)(2,1)} %refs_0_.15) | copy-start | bytes 786436
  22.9 9.2 %collective-permute-start.4 = (bf16[2,1024,128]{2,1,0:T(8,128)(2,1)S(1)}, bf16[2,1024,128]{2,1,0:T(8,128)(2,1)S(1)}, u32[]{:S(2)}, u32[]{:S(2)}) collective-permute-start(bf16[2,1024,128]{2,1,0:T(8,128)(2,1)S(1)} %collective-permute-done.3.refs_4_), channel_id=1, source_target_pairs={{0,8},{4,60},{8,16},{12,4},{16,24},{20,12},{24,32},{28,20},{32,40}... | collective-permute-start | bytes 1572872 | tf_op jit(solution)/shard_map/ppermute | solution.py:253
  26.7 11.1 %collective-permute-start.7 = (bf16[2,1024,128]{2,1,0:T(8,128)(2,1)S(1)}, bf16[2,1024,128]{2,1,0:T(8,128)(2,1)S(1)}, u32[]{:S(2)}, u32[]{:S(2)}) collective-permute-start(bf16[2,1024,128]{2,1,0:T(8,128)(2,1)S(1)} %collective-permute-done.5.refs_4_), channel_id=1, source_target_pairs={{0,8},{4,60},{8,16},{12,4},{16,24},{20,12},{24,32},{28,20},{32,40}... | collective-permute-start | bytes 1572872 | tf_op jit(solution)/shard_map/ppermute | solution.py:253
  32.1 11.2 %collective-permute-start.6 = (bf16[2,1024,128]{2,1,0:T(8,128)(2,1)S(1)}, bf16[2,1024,128]{2,1,0:T(8,128)(2,1)S(1)}, u32[]{:S(2)}, u32[]{:S(2)}) collective-permute-start(bf16[2,1024,128]{2,1,0:T(8,128)(2,1)S(1)} %collective-permute-done.4.refs_4_), channel_id=1, source_target_pairs={{0,8},{4,60},{8,16},{12,4},{16,24},{20,12},{24,32},{28,20},{32,40}... | collective-permute-start | bytes 1572872 | tf_op jit(solution)/shard_map/ppermute | solution.py:253
  37.7 11.2 %collective-permute-start.9 = (bf16[2,1024,128]{2,1,0:T(8,128)(2,1)S(1)}, bf16[2,1024,128]{2,1,0:T(8,128)(2,1)S(1)}, u32[]{:S(2)}, u32[]{:S(2)}) collective-permute-start(bf16[2,1024,128]{2,1,0:T(8,128)(2,1)S(1)} %collective-permute-done.7.refs_4_), channel_id=1, source_target_pairs={{0,8},{4,60},{8,16},{12,4},{16,24},{20,12},{24,32},{28,20},{32,40}... | collective-permute-start | bytes 1572872 | tf_op jit(solution)/shard_map/ppermute | solution.py:253
  43.3 11.2 %collective-permute-start.8 = (bf16[2,1024,128]{2,1,0:T(8,128)(2,1)S(1)}, bf16[2,1024,128]{2,1,0:T(8,128)(2,1)S(1)}, u32[]{:S(2)}, u32[]{:S(2)}) collective-permute-start(bf16[2,1024,128]{2,1,0:T(8,128)(2,1)S(1)} %collective-permute-done.6.refs_4_), channel_id=1, source_target_pairs={{0,8},{4,60},{8,16},{12,4},{16,24},{20,12},{24,32},{28,20},{32,40}... | collective-permute-start | bytes 1572872 | tf_op jit(solution)/shard_map/ppermute | solution.py:253
  55.5 6.1 %collective-permute-start.11 = (bf16[1072,128]{1,0:T(8,128)(2,1)S(1)}, bf16[1072,128]{1,0:T(8,128)(2,1)S(1)}, u32[]{:S(2)}, u32[]{:S(2)}) collective-permute-start(bf16[1072,128]{1,0:T(8,128)(2,1)S(1)} %leave_next.1), channel_id=1, source_target_pairs={{0,4},{4,0},{8,12},{12,8},{16,20},{20,16},{24,28},{28,24},{32,36},... | collective-permute-start | bytes 823304 | tf_op jit(solution)/shard_map/ppermute | solution.py:253
  60.6 1.8 %collective-permute-start.10 = (bf16[1072,128]{1,0:T(8,128)(2,1)S(1)}, bf16[1072,128]{1,0:T(8,128)(2,1)S(1)}, u32[]{:S(2)}, u32[]{:S(2)}) collective-permute-start(bf16[1072,128]{1,0:T(8,128)(2,1)S(1)} %leave_own.1), channel_id=1, source_target_pairs={{0,4},{4,0},{8,12},{12,8},{16,20},{20,16},{24,28},{28,24},{32,36},... | collective-permute-start | bytes 823304 | tf_op jit(solution)/shard_map/ppermute | solution.py:253
  62.3 24.7 %copy-start = (bf16[512,1536]{1,0:T(8,128)(2,1)S(1)}, bf16[512,1536]{1,0:T(8,128)(2,1)}, u32[]{:S(2)}) copy-start(bf16[512,1536]{1,0:T(8,128)(2,1)} %weight.1) | copy-start | bytes 4718596
  62.3 9.1 %collective-permute-start.12 = (bf16[1072,128]{1,0:T(8,128)(2,1)S(1)}, bf16[1072,128]{1,0:T(8,128)(2,1)S(1)}, u32[]{:S(2)}, u32[]{:S(2)}) collective-permute-start(bf16[1072,128]{1,0:T(8,128)(2,1)S(1)} %pass_on.1), channel_id=1, source_target_pairs={{0,64},{4,68},{8,72},{12,76},{16,80},{20,84},{24,88},{28,92},{32,9... | collective-permute-start | bytes 823304 | tf_op jit(solution)/shard_map/ppermute | solution.py:253
  72.4 8.2 %collective-permute-start.15 = (bf16[1024,128]{1,0:T(8,128)(2,1)S(1)}, bf16[1024,128]{1,0:T(8,128)(2,1)S(1)}, u32[]{:S(2)}, u32[]{:S(2)}) collective-permute-start(bf16[1024,128]{1,0:T(8,128)(2,1)S(1)} %join.1.own), channel_id=1, source_target_pairs={{0,2},{1,3},{2,0},{3,1},{4,6},{5,7},{6,4},{7,5},{8,10},{9,11},{10,... | collective-permute-start | bytes 786440 | tf_op jit(solution)/shard_map/ppermute | solution.py:275
  75.2 11.7 %collective-permute-start.14 = (bf16[1024,128]{1,0:T(8,128)(2,1)S(1)}, bf16[1024,128]{1,0:T(8,128)(2,1)S(1)}, u32[]{:S(2)}, u32[]{:S(2)}) collective-permute-start(bf16[1024,128]{1,0:T(8,128)(2,1)S(1)} %join.1.own), channel_id=1, source_target_pairs={{0,3},{1,0},{2,1},{3,2},{4,7},{5,4},{6,5},{7,6},{8,11},{9,8},{10,9... | collective-permute-start | bytes 786440 | tf_op jit(solution)/shard_map/ppermute | solution.py:275
  76.1 11.0 %collective-permute-start.13 = (bf16[1024,128]{1,0:T(8,128)(2,1)S(1)}, bf16[1024,128]{1,0:T(8,128)(2,1)S(1)}, u32[]{:S(2)}, u32[]{:S(2)}) collective-permute-start(bf16[1024,128]{1,0:T(8,128)(2,1)S(1)} %join.1.own), channel_id=1, source_target_pairs={{0,1},{1,2},{2,3},{3,0},{4,5},{5,6},{6,7},{7,4},{8,9},{9,10},{10,1... | collective-permute-start | bytes 786440 | tf_op jit(solution)/shard_map/ppermute | solution.py:275
where the time goes:
time: 91.6 us; the launch traced here: 90.7 us
  waiting for transfers between devices  39.4 us (43%)
  starting transfers between devices  32.8 us (36%)
  Pallas kernels  14.8 us (16%)
  other arithmetic  2.3 us (3%)
  local copies, waits for them, and re-layouts  1.04 us (1%)
    ppermute x13, waiting for transfers between devices, send(): lax.ppermute(value, 'ctx', [(i, target(i)) for i in range(ctx_count)])  29.1 us
    ppermute x13, starting transfers between devices, send(): lax.ppermute(value, 'ctx', [(i, target(i)) for i in range(ctx_count)])  28.6 us
    ppermute x3, waiting for transfers between devices, turn(): return lax.ppermute(value, 'head', pairs)  10.3 us
    pallas_call x10, Pallas kernels, fold(): pl.pallas_call(functools.partial(fold_kernel, first, parts), out_shape=sh...  9.04 us
    ppermute x3, starting transfers between devices, turn(): return lax.ppermute(value, 'head', pairs)  4.3 us
    pallas_call x1, Pallas kernels, project(): pl.pallas_call(project_kernel, grid=(steps,), out_shape=jax.ShapeDtypeStr...  3.62 us
    pallas_call x4, Pallas kernels, small_call(): pl.pallas_call(kernel, out_shape=out_shape, in_specs=[vmem_spec()] * len(...  2.12 us
  transfers between devices with their start and end apart: 16, of which 11 were waited for; matrix products, arithmetic and copies ran while one was open for 3% of the time, Pallas kernels for 10%

commit v1 on v0

--- a/solution.py
+++ b/solution.py
@@ -14,7 +14,6 @@
 START = -1e25
 TO_LOG2 = math.log2(math.e) * HEAD_DIM**-0.5
 VMEM_LIMIT = 16 * 2**20
-KEY_TILE = 256
 RING_CHIPS = 8
 
 
@@ -58,42 +57,48 @@
 
     @pl.loop(parts[0], parts[0] + count)
     def _(part):
-        rows = pl.ds(pl.multiple_of(part * tok, tok), tok)
         q_base = info[part]
         begin = [info[4 + part * blocks + i] for i in range(blocks)]
 
         @pl.when(wants(part))
         def _():
-            q = q_all[part - parts[0]]
-            m = m_in[rows, :]
-            acc = a_in[rows, :]
-            for t in range(tok // KEY_TILE):
-                keys = slice(t * KEY_TILE, (t + 1) * KEY_TILE)
-                s = lax.dot_general(
-                    q, kv[0, keys, :], (((1,), (1,)), ((), ())), preferred_element_type=jnp.float32
+            half = tok // 2
+            both = (slice(0, half), slice(half, tok))
+
+            def score(rows_in):
+                return lax.dot_general(
+                    q_all[part - parts[0], rows_in, :],
+                    kv[0],
+                    (((1,), (1,)), ((), ())),
+                    preferred_element_type=jnp.float32,
                 )
+
+            scores = [score(rows_in) for rows_in in both]
+            for n, s in enumerate(scores):
+                rows_here = pl.ds(pl.multiple_of(part * tok + n * half, half), half)
                 columns = []
-                for j in range(KEY_TILE // BLOCK):
-                    k_blk = k_base + t * (KEY_TILE // BLOCK) + j
+                for j in range(blocks):
                     column = []
-                    for i in range(blocks):
-                        seen = (k_blk >= begin[i]) & (k_blk <= q_base + i)
+                    for i in range(blocks // 2):
+                        i_all = n * (blocks // 2) + i
+                        seen = (k_base + j >= begin[i_all]) & (k_base + j <= q_base + i_all)
                         bias = jnp.where(seen, 0.0, FAR).astype(jnp.float32)
                         column.append(
                             s[i * BLOCK : (i + 1) * BLOCK, j * BLOCK : (j + 1) * BLOCK] + bias
                         )
                     columns.append(jnp.concatenate(column, axis=0))
                 s = jnp.concatenate(columns, axis=1)
+                m = m_in[rows_here, :]
                 new_m = jnp.maximum(m, jnp.max(s, axis=1, keepdims=True) * TO_LOG2)
                 factor = jnp.exp2(m - new_m)
-                p = jnp.exp2(s * TO_LOG2 - jnp.concatenate([new_m] * (KEY_TILE // HEAD_DIM), axis=1))
+                p = jnp.exp2(s * TO_LOG2 - jnp.concatenate([new_m] * blocks, axis=1))
                 added = jnp.dot(
-                    p.astype(jnp.bfloat16), v_wide[keys, :], preferred_element_type=jnp.float32
+                    p.astype(jnp.bfloat16), v_wide[...], preferred_element_type=jnp.float32
                 )
-                acc = acc * jnp.concatenate([factor] * 2, axis=1) + added
-                m = new_m
-            m_out[rows, :] = m
-            a_out[rows, :] = acc
+                a_out[rows_here, :] = (
+                    a_in[rows_here, :] * jnp.concatenate([factor] * 2, axis=1) + added
+                )
+                m_out[rows_here, :] = new_m
 
 
 def fold(info, key_base, q_parts, parts, kv, state, weight=46):
@@ -203,7 +208,7 @@
     )(*args)
 
 
-def project_kernel(heads, own, left, right, far, weight, out_ref, lhs):
+def project_kernel(heads, own, left, right, far_a, far_b, weight, out_ref, lhs):
     step = pl.program_id(0)
     h = heads[0]
     count = weight.shape[0] // HEAD_DIM
@@ -211,9 +216,16 @@
 
     @pl.when(step == 0)
     def _():
-        for by, piece in ((0, own), (count - 1, left), (1, right), (2, far)):
+        half = far_a.shape[0]
+        for by, piece, rows in (
+            (0, own, slice(0, 2 * half)),
+            (count - 1, left, slice(0, 2 * half)),
+            (1, right, slice(0, 2 * half)),
+            (2, far_a, slice(0, half)),
+            (2, far_b, slice(half, 2 * half)),
+        ):
             column = pl.multiple_of(lax.rem(h + by, count) * HEAD_DIM, HEAD_DIM)
-            lhs[:, pl.ds(column, HEAD_DIM)] = piece[...]
+            lhs[rows, pl.ds(column, HEAD_DIM)] = piece[...]
 
     columns = pl.ds(pl.multiple_of(step * width, width), width)
     out_ref[...] = jnp.dot(
@@ -229,7 +241,7 @@
         project_kernel,
         grid=(steps,),
         out_shape=jax.ShapeDtypeStruct((tok, weight.shape[1]), jnp.bfloat16),
-        in_specs=[smem_spec()] + [vmem_spec()] * 5,
+        in_specs=[smem_spec()] + [vmem_spec()] * 6,
         out_specs=pl.BlockSpec((tok, width), lambda i: (0, i)),
         scratch_shapes=[pltpu.VMEM((tok, weight.shape[0]), jnp.bfloat16)],
         compiler_params=pltpu.CompilerParams(vmem_limit_bytes=VMEM_LIMIT),
@@ -274,12 +286,6 @@
         pairs = [(i, (i + by) % head_count) for i in range(head_count)]
         return lax.ppermute(value, "head", pairs)
 
-    kv = jnp.stack([key_states, value_states])
-    near = send(kv, along)
-    cross = send(kv, lambda i: along(sibling(i)))
-    next_own = send(queries, down)
-    q_sibling = send(queries, sibling)
-
     upto = jnp.arange(clip_lengths.shape[0])
     ends = jnp.sum(jnp.where(upto[None, :] <= upto[:, None], clip_lengths[None, :], 0), axis=1)
     owners = jnp.stack([me, me ^ 1, (me + ring) % ctx_count, ((me + ring) % ctx_count) ^ 1])
@@ -289,6 +295,13 @@
         jnp.where(ends[None, None, :] <= q_blocks[:, :, None], ends[None, None, :], 0), axis=-1
     )
     info = jnp.concatenate([bases, begin.reshape(-1)]).astype(jnp.int32)
+
+    kv = jnp.stack([key_states, value_states])
+    near = send(kv, along)
+    kv, info = lax.optimization_barrier((kv, info))
+    cross = send(kv, lambda i: along(sibling(i)))
+    next_own = send(queries, down)
+    q_sibling = send(queries, sibling)
 
     def base_of(step, of_core):
         chip = (place + jnp.where(core == 0, -step, step)) % RING_CHIPS
@@ -331,7 +344,14 @@
         own_there,
         back,
     )
-    pieces = (attended, turn(attended, 1), turn(attended, -1), turn(attended, 2))
+    half = tok // 2
+    pieces = (
+        attended,
+        turn(attended, 1),
+        turn(attended, -1),
+        turn(attended[:half], 2),
+        turn(attended[half:], -2),
+    )
     return project(head.reshape(1).astype(jnp.int32), pieces, out_weight)
 
 

time: 91.6 us -> 90.3 us (0.986)
  the two profiles are of different devices: /device:TPU:1 before, /device:TPU:128 now
where the time goes in v1:
time: 90.3 us; the launch traced here: 89.2 us
  Pallas kernels  40.4 us (45%)
  waiting for transfers between devices  30.9 us (34%)
  starting transfers between devices  14.3 us (16%)
  other arithmetic  2.3 us (3%)
  local copies, waits for them, and re-layouts  1.09 us (1%)
    pallas_call x10, Pallas kernels, fold(): pl.pallas_call(functools.partial(fold_kernel, first, parts), out_shape=sh...  34.6 us
    ppermute x13, waiting for transfers between devices, send(): lax.ppermute(value, 'ctx', [(i, target(i)) for i in range(ctx_count)])  20.5 us
    ppermute x4, waiting for transfers between devices, turn(): return lax.ppermute(value, 'head', pairs)  10.4 us
    ppermute x13, starting transfers between devices, send(): lax.ppermute(value, 'ctx', [(i, target(i)) for i in range(ctx_count)])  7.87 us
    ppermute x4, starting transfers between devices, turn(): return lax.ppermute(value, 'head', pairs)  6.46 us
    pallas_call x1, Pallas kernels, project(): pl.pallas_call(project_kernel, grid=(steps,), out_shape=jax.ShapeDtypeStr...  3.63 us
    pallas_call x4, Pallas kernels, small_call(): pl.pallas_call(kernel, out_shape=out_shape, in_specs=[vmem_spec()] * len(...  2.12 us
  transfers between devices with their start and end apart: 17, of which 11 were waited for; matrix products, arithmetic and copies ran while one was open for 1% of the time, Pallas kernels for 35%

profile of v1, /device:TPU:128, one launch (start us, length us, event | category | flops | bytes accessed | tf_op | source)
XLA Modules:
  0.0 89.2 jit_solution(9496313879922765230)
XLA Ops:
  0.0 1.1 %pad_maximum_fusion.refs_1_.refs_2_ = bf16[2,1024,128]{2,1,0:T(8,128)(2,1)S(1)} fusion(bf16[1,1024,128]{2,1,0:T(8,128)(2,1)} %bitcast.15, bf16[1,1024,128]{2,1,0:T(8,128)(2,1)} %bitcast.16), kind=kLoop, calls=%fused_computation | loop fusion | flops 262144 | bytes 1048576 | tf_op jit(solution)/shard_map/stack | solution.py:299
  1.1 1.1 %collective-permute-start.3 = (bf16[2,1024,128]{2,1,0:T(8,128)(2,1)S(1)}, bf16[2,1024,128]{2,1,0:T(8,128)(2,1)S(1)}, u32[]{:S(2)}, u32[]{:S(2)}) collective-permute-start(bf16[2,1024,128]{2,1,0:T(8,128)(2,1)S(1)} %pad_maximum_fusion.refs_1_.refs_2_), channel_id=1, source_target_pairs={{0,8},{4,60},{8,16},{12,4},{16,24},{20,12},{24,32},{28,20},{32,40}... | collective-permute-start | bytes 1572872 | tf_op jit(solution)/shard_map/ppermute | solution.py:265
  2.2 0.8 select_reduce_fusion.1
  2.9 0.1 add_multiply_fusion
  3.0 0.1 iota_add_fusion
  3.1 0.2 select_reduce_fusion
  3.3 0.1 reshape.86
  3.4 0.1 pad_add_fusion.info
  3.5 1.1 %collective-permute-start = (bf16[1024,128]{1,0:T(8,128)(2,1)}, bf16[1024,128]{1,0:T(8,128)(2,1)S(1)}, u32[]{:S(2)}, u32[]{:S(2)}) collective-permute-start(bf16[1024,128]{1,0:T(8,128)(2,1)} %refs_0_.15), channel_id=1, source_target_pairs={{0,4},{4,0},{8,12},{12,8},{16,20},{20,16},{24,28},{28,24},{32,36},... | collective-permute-start | bytes 786440 | tf_op jit(solution)/shard_map/ppermute | solution.py:265
  4.6 2.6 %collective-permute-start.2 = (bf16[1024,128]{1,0:T(8,128)(2,1)}, bf16[1024,128]{1,0:T(8,128)(2,1)S(1)}, u32[]{:S(2)}, u32[]{:S(2)}) collective-permute-start(bf16[1024,128]{1,0:T(8,128)(2,1)} %refs_0_.15), channel_id=1, source_target_pairs={{0,196},{4,192},{8,204},{12,200},{16,212},{20,208},{24,220},{28,21... | collective-permute-start | bytes 786440 | tf_op jit(solution)/shard_map/ppermute | solution.py:265
  7.3 0.7 collective-permute-start.1
  8.0 1.0 %copy-done.1 = bf16[1024,128]{1,0:T(8,128)(2,1)S(1)} copy-done((bf16[1024,128]{1,0:T(8,128)(2,1)S(1)}, bf16[1024,128]{1,0:T(8,128)(2,1)}, u32[]{:S(2)}) %copy-start.1) | copy-done | bytes 262168
  9.0 2.6 %fold.10 = (f32[4096,128]{1,0:T(8,128)S(1)}, f32[4096,256]{1,0:T(8,128)S(1)}) custom-call(s32[36]{0:T(128)S(1)} %pad_add_fusion.info, s32[1]{0:T(128)} %bitcast.8.key_base, bf16[1024,128]{1,0:T(8,128)(2,1)S(1)} %copy-done.1, bf16[2,1024,128]{2,1,0:T(8,128)(2,1)S(1)} %pad_maximum_fusion.refs_1_.refs_2_), custom_call_target="tpu_custom_call" | custom-call | flops 536870912 | bytes 1000000 | tf_op jit(solution)/shard_map/fold/pallas_call | solution.py:112
  11.6 2.7 %fold.11 = (f32[4096,128]{1,0:T(8,128)S(1)}, f32[4096,256]{1,0:T(8,128)S(1)}) custom-call(s32[36]{0:T(128)S(1)} %pad_add_fusion.info, s32[1]{0:T(128)} %bitcast.8.key_base, bf16[1024,128]{1,0:T(8,128)(2,1)S(1)} %collective-permute-done.refs_0_.refs_1_, ...), custom_call_target="tpu_custom_call", output_to_operand_aliasing={{0}: (4, {}), {1}: (5, {})} | custom-call | flops 536870912 | bytes 1000000 | tf_op jit(solution)/shard_map/fold/pallas_call | solution.py:112
  14.3 1.0 %collective-permute-done.3.refs_4_ = bf16[2,1024,128]{2,1,0:T(8,128)(2,1)S(1)} collective-permute-done((bf16[2,1024,128]{2,1,0:T(8,128)(2,1)S(1)}, bf16[2,1024,128]{2,1,0:T(8,128)(2,1)S(1)}, u32[]{:S(2)}, u32[]{:S(2)}) %collective-permute-start.3) | collective-permute-done | bytes 524320 | tf_op jit(solution)/shard_map/ppermute | solution.py:265
  15.3 0.1 collective-permute-start.4
  15.4 4.3 %collective-permute-done.1.refs_2_.refs_0_ = bf16[1024,128]{1,0:T(8,128)(2,1)S(1)} collective-permute-done((bf16[1024,128]{1,0:T(8,128)(2,1)}, bf16[1024,128]{1,0:T(8,128)(2,1)S(1)}, u32[]{:S(2)}, u32[]{:S(2)}) %collective-permute-start.1) | collective-permute-done | bytes 262176 | tf_op jit(solution)/shard_map/ppermute | solution.py:265
  19.7 4.0 %fold.12 = (f32[4096,128]{1,0:T(8,128)S(1)}, f32[4096,256]{1,0:T(8,128)S(1)}) custom-call(s32[36]{0:T(128)S(1)} %pad_add_fusion.info, s32[1]{0:T(128)} %bitcast.10.key_base, bf16[1024,128]{1,0:T(8,128)(2,1)S(1)} %copy-done.1, bf16[1024,128]{1,0:T(8,128)(2,1)S(1)} %collective-permute-done.refs_0_.refs_1_, ...), custom_call_target="tpu_custom_call", output_to_operand_aliasing={{0}: (7, {}), {1}: (8, {})} | custom-call | flops 1073741824 | bytes 1000000 | tf_op jit(solution)/shard_map/fold/pallas_call | solution.py:112
  23.8 1.1 %collective-permute-start.7 = (bf16[2,1024,128]{2,1,0:T(8,128)(2,1)S(1)}, bf16[2,1024,128]{2,1,0:T(8,128)(2,1)S(1)}, u32[]{:S(2)}, u32[]{:S(2)}) collective-permute-start(bf16[2,1024,128]{2,1,0:T(8,128)(2,1)S(1)} %collective-permute-done.5.refs_4_), channel_id=1, source_target_pairs={{0,8},{4,60},{8,16},{12,4},{16,24},{20,12},{24,32},{28,20},{32,40}... | collective-permute-start | bytes 1572872 | tf_op jit(solution)/shard_map/ppermute | solution.py:265
  24.9 4.2 %fold.13 = (f32[4096,128]{1,0:T(8,128)S(1)}, f32[4096,256]{1,0:T(8,128)S(1)}) custom-call(s32[36]{0:T(128)S(1)} %pad_add_fusion.info, s32[1]{0:T(128)} %bitcast.9.key_base, bf16[1024,128]{1,0:T(8,128)(2,1)S(1)} %copy-done.1, bf16[1024,128]{1,0:T(8,128)(2,1)S(1)} %collective-permute-done.refs_0_.refs_1_, ...), custom_call_target="tpu_custom_call", output_to_operand_aliasing={{0}: (7, {}), {1}: (8, {})} | custom-call | flops 6174015488 | bytes 1000000 | tf_op jit(solution)/shard_map/fold/pallas_call | solution.py:112
  29.1 0.2 collective-permute-start.6
  29.3 4.1 %fold.14 = (f32[4096,128]{1,0:T(8,128)S(1)}, f32[4096,256]{1,0:T(8,128)S(1)}) custom-call(s32[36]{0:T(128)S(1)} %pad_add_fusion.info, s32[1]{0:T(128)} %bitcast.12.key_base, bf16[1024,128]{1,0:T(8,128)(2,1)S(1)} %copy-done.1, bf16[1024,128]{1,0:T(8,128)(2,1)S(1)} %collective-permute-done.refs_0_.refs_1_, ...), custom_call_target="tpu_custom_call", output_to_operand_aliasing={{0}: (7, {}), {1}: (8, {})} | custom-call | flops 6174015488 | bytes 1000000 | tf_op jit(solution)/shard_map/fold/pallas_call | solution.py:112
  33.3 0.9 %collective-permute-done.7.refs_4_ = bf16[2,1024,128]{2,1,0:T(8,128)(2,1)S(1)} collective-permute-done((bf16[2,1024,128]{2,1,0:T(8,128)(2,1)S(1)}, bf16[2,1024,128]{2,1,0:T(8,128)(2,1)S(1)}, u32[]{:S(2)}, u32[]{:S(2)}) %collective-permute-start.7) | collective-permute-done | bytes 524320 | tf_op jit(solution)/shard_map/ppermute | solution.py:265
  34.2 0.2 collective-permute-start.9
  34.4 4.1 %fold.15 = (f32[4096,128]{1,0:T(8,128)S(1)}, f32[4096,256]{1,0:T(8,128)S(1)}) custom-call(s32[36]{0:T(128)S(1)} %pad_add_fusion.info, s32[1]{0:T(128)} %bitcast.11.key_base, bf16[1024,128]{1,0:T(8,128)(2,1)S(1)} %copy-done.1, bf16[1024,128]{1,0:T(8,128)(2,1)S(1)} %collective-permute-done.refs_0_.refs_1_, ...), custom_call_target="tpu_custom_call", output_to_operand_aliasing={{0}: (7, {}), {1}: (8, {})} | custom-call | flops 6174015488 | bytes 1000000 | tf_op jit(solution)/shard_map/fold/pallas_call | solution.py:112
  38.5 1.4 %collective-permute-done.6.refs_4_ = bf16[2,1024,128]{2,1,0:T(8,128)(2,1)S(1)} collective-permute-done((bf16[2,1024,128]{2,1,0:T(8,128)(2,1)S(1)}, bf16[2,1024,128]{2,1,0:T(8,128)(2,1)S(1)}, u32[]{:S(2)}, u32[]{:S(2)}) %collective-permute-start.6) | collective-permute-done | bytes 524320 | tf_op jit(solution)/shard_map/ppermute | solution.py:265
  39.9 4.0 %fold.16 = (f32[4096,128]{1,0:T(8,128)S(1)}, f32[4096,256]{1,0:T(8,128)S(1)}) custom-call(s32[36]{0:T(128)S(1)} %pad_add_fusion.info, s32[1]{0:T(128)} %bitcast.14.key_base, bf16[1024,128]{1,0:T(8,128)(2,1)S(1)} %copy-done.1, bf16[1024,128]{1,0:T(8,128)(2,1)S(1)} %collective-permute-done.refs_0_.refs_1_, ...), custom_call_target="tpu_custom_call", output_to_operand_aliasing={{0}: (7, {}), {1}: (8, {})} | custom-call | flops 6174015488 | bytes 1000000 | tf_op jit(solution)/shard_map/fold/pallas_call | solution.py:112
  43.9 1.6 %collective-permute-done.9.refs_4_ = bf16[2,1024,128]{2,1,0:T(8,128)(2,1)S(1)} collective-permute-done((bf16[2,1024,128]{2,1,0:T(8,128)(2,1)S(1)}, bf16[2,1024,128]{2,1,0:T(8,128)(2,1)S(1)}, u32[]{:S(2)}, u32[]{:S(2)}) %collective-permute-start.9) | collective-permute-done | bytes 524320 | tf_op jit(solution)/shard_map/ppermute | solution.py:265
  45.5 4.1 %fold.17 = (f32[4096,128]{1,0:T(8,128)S(1)}, f32[4096,256]{1,0:T(8,128)S(1)}) custom-call(s32[36]{0:T(128)S(1)} %pad_add_fusion.info, s32[1]{0:T(128)} %bitcast.13.key_base, bf16[1024,128]{1,0:T(8,128)(2,1)S(1)} %copy-done.1, bf16[1024,128]{1,0:T(8,128)(2,1)S(1)} %collective-permute-done.refs_0_.refs_1_, ...), custom_call_target="tpu_custom_call", output_to_operand_aliasing={{0}: (7, {}), {1}: (8, {})} | custom-call | flops 6174015488 | bytes 1000000 | tf_op jit(solution)/shard_map/fold/pallas_call | solution.py:112
  49.5 0.8 fold.18
  50.4 0.7 collective-permute-done.8.refs_4_
  51.1 4.1 %fold.19 = (f32[4096,128]{1,0:T(8,128)S(1)}, f32[4096,256]{1,0:T(8,128)S(1)}) custom-call(s32[36]{0:T(128)S(1)} %pad_add_fusion.info, s32[1]{0:T(128)} %bitcast.7.key_base, bf16[1024,128]{1,0:T(8,128)(2,1)S(1)} %copy-done.1, bf16[1024,128]{1,0:T(8,128)(2,1)S(1)} %collective-permute-done.refs_0_.refs_1_, ...), custom_call_target="tpu_custom_call", output_to_operand_aliasing={{0}: (7, {}), {1}: (8, {})} | custom-call | flops 6174015488 | bytes 1000000 | tf_op jit(solution)/shard_map/fold/pallas_call | solution.py:112
  55.2 0.2 leave_next.1
  55.4 0.1 collective-permute-start.11
  55.5 0.2 leave_own.1
  55.7 0.6 collective-permute-start.10
  56.3 0.8 collective-permute-done.11.other
  57.0 0.7 pass_on.1
  57.7 0.1 collective-permute-start.12
  57.9 9.8 %collective-permute-done.12.back = bf16[1072,128]{1,0:T(8,128)(2,1)S(1)} collective-permute-done((bf16[1072,128]{1,0:T(8,128)(2,1)S(1)}, bf16[1072,128]{1,0:T(8,128)(2,1)S(1)}, u32[]{:S(2)}, u32[]{:S(2)}) %collective-permute-start.12) | collective-permute-done | bytes 274464 | tf_op jit(solution)/shard_map/ppermute | solution.py:265
  67.6 1.0 %join.1.own = bf16[1024,128]{1,0:T(8,128)(2,1)S(1)} custom-call(f32[4096,128]{1,0:T(8,128)S(1)} %get-tuple-element.67.m_ref, f32[4096,256]{1,0:T(8,128)S(1)} %get-tuple-element.68.a_ref, bf16[1072,128]{1,0:T(8,128)(2,1)S(1)} %collective-permute-done.10.other, bf16[1072,128]{1,0:T(8,128)(2,1)S(1)} %collective-permute-done.12.back), custom_call_target="tpu_custom_call" | custom-call | tf_op jit(solution)/shard_map/join/pallas_call | solution.py:201
  68.6 2.8 %collective-permute-start.14 = (bf16[1024,128]{1,0:T(8,128)(2,1)S(1)}, bf16[1024,128]{1,0:T(8,128)(2,1)S(1)}, u32[]{:S(2)}, u32[]{:S(2)}) collective-permute-start(bf16[1024,128]{1,0:T(8,128)(2,1)S(1)} %join.1.own), channel_id=1, source_target_pairs={{0,3},{1,0},{2,1},{3,2},{4,7},{5,4},{6,5},{7,6},{8,11},{9,8},{10,9... | collective-permute-start | bytes 786440 | tf_op jit(solution)/shard_map/ppermute | solution.py:287
  71.5 2.4 %collective-permute-start.16 = (bf16[512,128]{1,0:T(8,128)(2,1)S(1)}, bf16[512,128]{1,0:T(8,128)(2,1)S(1)}, u32[]{:S(2)}, u32[]{:S(2)}) collective-permute-start(bf16[512,128]{1,0:T(8,128)(2,1)S(1)} %get-tuple-element.69), channel_id=1, source_target_pairs={{0,2},{1,3},{2,0},{3,1},{4,6},{5,7},{6,4},{7,5},{8,10},{9,11},{10,... | collective-permute-start | bytes 393224 | tf_op jit(solution)/shard_map/ppermute | solution.py:287
  73.9 1.2 %collective-permute-start.15 = (bf16[512,128]{1,0:T(8,128)(2,1)S(1)}, bf16[512,128]{1,0:T(8,128)(2,1)S(1)}, u32[]{:S(2)}, u32[]{:S(2)}) collective-permute-start(bf16[512,128]{1,0:T(8,128)(2,1)S(1)} %get-tuple-element.70), channel_id=1, source_target_pairs={{0,2},{1,3},{2,0},{3,1},{4,6},{5,7},{6,4},{7,5},{8,10},{9,11},{10,... | collective-permute-start | bytes 393224 | tf_op jit(solution)/shard_map/ppermute | solution.py:287
  75.1 8.2 %collective-permute-done.16.far_b = bf16[512,128]{1,0:T(8,128)(2,1)S(1)} collective-permute-done((bf16[512,128]{1,0:T(8,128)(2,1)S(1)}, bf16[512,128]{1,0:T(8,128)(2,1)S(1)}, u32[]{:S(2)}, u32[]{:S(2)}) %collective-permute-start.16) | collective-permute-done | bytes 131104 | tf_op jit(solution)/shard_map/ppermute | solution.py:287
  83.3 1.4 %collective-permute-done.15.far_a = bf16[512,128]{1,0:T(8,128)(2,1)S(1)} collective-permute-done((bf16[512,128]{1,0:T(8,128)(2,1)S(1)}, bf16[512,128]{1,0:T(8,128)(2,1)S(1)}, u32[]{:S(2)}, u32[]{:S(2)}) %collective-permute-start.15) | collective-permute-done | bytes 131104 | tf_op jit(solution)/shard_map/ppermute | solution.py:287
  84.7 0.8 collective-permute-done.13.left
  85.5 3.6 %project.1 = bf16[1024,1536]{1,0:T(8,128)(2,1)} custom-call(s32[1]{0:T(128)} %bitcast.heads, bf16[1024,128]{1,0:T(8,128)(2,1)S(1)} %join.1.own, bf16[1024,128]{1,0:T(8,128)(2,1)S(1)} %collective-permute-done.13.left, bf16[1024,128]{1,0:T(8,128)(2,1)S(1)} %collective-permute-done.14.right, bf16[512,128]{1,0:T(8,128)(2,1)S(1)} %collective-permute-done.15.far_a, ...), custom_call_target="tpu_custom_call" | custom-call | tf_op jit(solution)/shard_map/project/pallas_call | solution.py:240
  (13 shorter events, 0.1 us)
Async XLA Ops:
  1.1 14.2 %collective-permute-start.3 = (bf16[2,1024,128]{2,1,0:T(8,128)(2,1)S(1)}, bf16[2,1024,128]{2,1,0:T(8,128)(2,1)S(1)}, u32[]{:S(2)}, u32[]{:S(2)}) collective-permute-start(bf16[2,1024,128]{2,1,0:T(8,128)(2,1)S(1)} %pad_maximum_fusion.refs_1_.refs_2_), channel_id=1, source_target_pairs={{0,8},{4,60},{8,16},{12,4},{16,24},{20,12},{24,32},{28,20},{32,40}... | collective-permute-start | bytes 1572872 | tf_op jit(solution)/shard_map/ppermute | solution.py:265
  3.5 20.3 %collective-permute-start.5 = (bf16[2,1024,128]{2,1,0:T(8,128)(2,1)S(1)}, bf16[2,1024,128]{2,1,0:T(8,128)(2,1)S(1)}, u32[]{:S(2)}, u32[]{:S(2)}) collective-permute-start(bf16[2,1024,128]{2,1,0:T(8,128)(2,1)S(1)} %pad_maximum_fusion.refs_1_.refs_2_), channel_id=1, source_target_pairs={{0,60},{4,8},{8,4},{12,16},{16,12},{20,24},{24,20},{28,32},{32,28}... | collective-permute-start | bytes 1572872 | tf_op jit(solution)/shard_map/ppermute | solution.py:265
  3.5 8.0 %collective-permute-start = (bf16[1024,128]{1,0:T(8,128)(2,1)}, bf16[1024,128]{1,0:T(8,128)(2,1)S(1)}, u32[]{:S(2)}, u32[]{:S(2)}) collective-permute-start(bf16[1024,128]{1,0:T(8,128)(2,1)} %refs_0_.15), channel_id=1, source_target_pairs={{0,4},{4,0},{8,12},{12,8},{16,20},{20,16},{24,28},{28,24},{32,36},... | collective-permute-start | bytes 786440 | tf_op jit(solution)/shard_map/ppermute | solution.py:265
  4.6 10.8 %collective-permute-start.2 = (bf16[1024,128]{1,0:T(8,128)(2,1)}, bf16[1024,128]{1,0:T(8,128)(2,1)S(1)}, u32[]{:S(2)}, u32[]{:S(2)}) collective-permute-start(bf16[1024,128]{1,0:T(8,128)(2,1)} %refs_0_.15), channel_id=1, source_target_pairs={{0,196},{4,192},{8,204},{12,200},{16,212},{20,208},{24,220},{28,21... | collective-permute-start | bytes 786440 | tf_op jit(solution)/shard_map/ppermute | solution.py:265
  7.3 12.5 %collective-permute-start.1 = (bf16[1024,128]{1,0:T(8,128)(2,1)}, bf16[1024,128]{1,0:T(8,128)(2,1)S(1)}, u32[]{:S(2)}, u32[]{:S(2)}) collective-permute-start(bf16[1024,128]{1,0:T(8,128)(2,1)} %refs_0_.15), channel_id=1, source_target_pairs={{0,192},{4,196},{8,200},{12,204},{16,208},{20,212},{24,216},{28,22... | collective-permute-start | bytes 786440 | tf_op jit(solution)/shard_map/ppermute | solution.py:265
  8.0 1.0 %copy-start.1 = (bf16[1024,128]{1,0:T(8,128)(2,1)S(1)}, bf16[1024,128]{1,0:T(8,128)(2,1)}, u32[]{:S(2)}) copy-start(bf16[1024,128]{1,0:T(8,128)(2,1)} %refs_0_.15) | copy-start | bytes 786436
  15.3 13.8 %collective-permute-start.4 = (bf16[2,1024,128]{2,1,0:T(8,128)(2,1)S(1)}, bf16[2,1024,128]{2,1,0:T(8,128)(2,1)S(1)}, u32[]{:S(2)}, u32[]{:S(2)}) collective-permute-start(bf16[2,1024,128]{2,1,0:T(8,128)(2,1)S(1)} %collective-permute-done.3.refs_4_), channel_id=1, source_target_pairs={{0,8},{4,60},{8,16},{12,4},{16,24},{20,12},{24,32},{28,20},{32,40}... | collective-permute-start | bytes 1572872 | tf_op jit(solution)/shard_map/ppermute | solution.py:265
  23.8 10.5 %collective-permute-start.7 = (bf16[2,1024,128]{2,1,0:T(8,128)(2,1)S(1)}, bf16[2,1024,128]{2,1,0:T(8,128)(2,1)S(1)}, u32[]{:S(2)}, u32[]{:S(2)}) collective-permute-start(bf16[2,1024,128]{2,1,0:T(8,128)(2,1)S(1)} %collective-permute-done.5.refs_4_), channel_id=1, source_target_pairs={{0,8},{4,60},{8,16},{12,4},{16,24},{20,12},{24,32},{28,20},{32,40}... | collective-permute-start | bytes 1572872 | tf_op jit(solution)/shard_map/ppermute | solution.py:265
  29.1 10.7 %collective-permute-start.6 = (bf16[2,1024,128]{2,1,0:T(8,128)(2,1)S(1)}, bf16[2,1024,128]{2,1,0:T(8,128)(2,1)S(1)}, u32[]{:S(2)}, u32[]{:S(2)}) collective-permute-start(bf16[2,1024,128]{2,1,0:T(8,128)(2,1)S(1)} %collective-permute-done.4.refs_4_), channel_id=1, source_target_pairs={{0,8},{4,60},{8,16},{12,4},{16,24},{20,12},{24,32},{28,20},{32,40}... | collective-permute-start | bytes 1572872 | tf_op jit(solution)/shard_map/ppermute | solution.py:265
  34.2 11.2 %collective-permute-start.9 = (bf16[2,1024,128]{2,1,0:T(8,128)(2,1)S(1)}, bf16[2,1024,128]{2,1,0:T(8,128)(2,1)S(1)}, u32[]{:S(2)}, u32[]{:S(2)}) collective-permute-start(bf16[2,1024,128]{2,1,0:T(8,128)(2,1)S(1)} %collective-permute-done.7.refs_4_), channel_id=1, source_target_pairs={{0,8},{4,60},{8,16},{12,4},{16,24},{20,12},{24,32},{28,20},{32,40}... | collective-permute-start | bytes 1572872 | tf_op jit(solution)/shard_map/ppermute | solution.py:265
  39.9 11.2 %collective-permute-start.8 = (bf16[2,1024,128]{2,1,0:T(8,128)(2,1)S(1)}, bf16[2,1024,128]{2,1,0:T(8,128)(2,1)S(1)}, u32[]{:S(2)}, u32[]{:S(2)}) collective-permute-start(bf16[2,1024,128]{2,1,0:T(8,128)(2,1)S(1)} %collective-permute-done.6.refs_4_), channel_id=1, source_target_pairs={{0,8},{4,60},{8,16},{12,4},{16,24},{20,12},{24,32},{28,20},{32,40}... | collective-permute-start | bytes 1572872 | tf_op jit(solution)/shard_map/ppermute | solution.py:265
  55.4 1.6 %collective-permute-start.11 = (bf16[1072,128]{1,0:T(8,128)(2,1)S(1)}, bf16[1072,128]{1,0:T(8,128)(2,1)S(1)}, u32[]{:S(2)}, u32[]{:S(2)}) collective-permute-start(bf16[1072,128]{1,0:T(8,128)(2,1)S(1)} %leave_next.1), channel_id=1, source_target_pairs={{0,4},{4,0},{8,12},{12,8},{16,20},{20,16},{24,28},{28,24},{32,36},... | collective-permute-start | bytes 823304 | tf_op jit(solution)/shard_map/ppermute | solution.py:265
  55.7 2.2 %collective-permute-start.10 = (bf16[1072,128]{1,0:T(8,128)(2,1)S(1)}, bf16[1072,128]{1,0:T(8,128)(2,1)S(1)}, u32[]{:S(2)}, u32[]{:S(2)}) collective-permute-start(bf16[1072,128]{1,0:T(8,128)(2,1)S(1)} %leave_own.1), channel_id=1, source_target_pairs={{0,4},{4,0},{8,12},{12,8},{16,20},{20,16},{24,28},{28,24},{32,36},... | collective-permute-start | bytes 823304 | tf_op jit(solution)/shard_map/ppermute | solution.py:265
  57.7 27.8 %copy-start = (bf16[512,1536]{1,0:T(8,128)(2,1)S(1)}, bf16[512,1536]{1,0:T(8,128)(2,1)}, u32[]{:S(2)}) copy-start(bf16[512,1536]{1,0:T(8,128)(2,1)} %weight.1) | copy-start | bytes 4718596
  57.7 9.9 %collective-permute-start.12 = (bf16[1072,128]{1,0:T(8,128)(2,1)S(1)}, bf16[1072,128]{1,0:T(8,128)(2,1)S(1)}, u32[]{:S(2)}, u32[]{:S(2)}) collective-permute-start(bf16[1072,128]{1,0:T(8,128)(2,1)S(1)} %pass_on.1), channel_id=1, source_target_pairs={{0,64},{4,68},{8,72},{12,76},{16,80},{20,84},{24,88},{28,92},{32,9... | collective-permute-start | bytes 823304 | tf_op jit(solution)/shard_map/ppermute | solution.py:265
  68.6 16.1 %collective-permute-start.14 = (bf16[1024,128]{1,0:T(8,128)(2,1)S(1)}, bf16[1024,128]{1,0:T(8,128)(2,1)S(1)}, u32[]{:S(2)}, u32[]{:S(2)}) collective-permute-start(bf16[1024,128]{1,0:T(8,128)(2,1)S(1)} %join.1.own), channel_id=1, source_target_pairs={{0,3},{1,0},{2,1},{3,2},{4,7},{5,4},{6,5},{7,6},{8,11},{9,8},{10,9... | collective-permute-start | bytes 786440 | tf_op jit(solution)/shard_map/ppermute | solution.py:287
  71.5 14.1 %collective-permute-start.13 = (bf16[1024,128]{1,0:T(8,128)(2,1)S(1)}, bf16[1024,128]{1,0:T(8,128)(2,1)S(1)}, u32[]{:S(2)}, u32[]{:S(2)}) collective-permute-start(bf16[1024,128]{1,0:T(8,128)(2,1)S(1)} %join.1.own), channel_id=1, source_target_pairs={{0,1},{1,2},{2,3},{3,0},{4,5},{5,6},{6,7},{7,4},{8,9},{9,10},{10,1... | collective-permute-start | bytes 786440 | tf_op jit(solution)/shard_map/ppermute | solution.py:287
  71.5 11.8 %collective-permute-start.16 = (bf16[512,128]{1,0:T(8,128)(2,1)S(1)}, bf16[512,128]{1,0:T(8,128)(2,1)S(1)}, u32[]{:S(2)}, u32[]{:S(2)}) collective-permute-start(bf16[512,128]{1,0:T(8,128)(2,1)S(1)} %get-tuple-element.69), channel_id=1, source_target_pairs={{0,2},{1,3},{2,0},{3,1},{4,6},{5,7},{6,4},{7,5},{8,10},{9,11},{10,... | collective-permute-start | bytes 393224 | tf_op jit(solution)/shard_map/ppermute | solution.py:287
  73.9 10.8 %collective-permute-start.15 = (bf16[512,128]{1,0:T(8,128)(2,1)S(1)}, bf16[512,128]{1,0:T(8,128)(2,1)S(1)}, u32[]{:S(2)}, u32[]{:S(2)}) collective-permute-start(bf16[512,128]{1,0:T(8,128)(2,1)S(1)} %get-tuple-element.70), channel_id=1, source_target_pairs={{0,2},{1,3},{2,0},{3,1},{4,6},{5,7},{6,4},{7,5},{8,10},{9,11},{10,... | collective-permute-start | bytes 393224 | tf_op jit(solution)/shard_map/ppermute | solution.py:287

commit v2 on v1

--- a/solution.py
+++ b/solution.py
@@ -286,6 +286,13 @@
         pairs = [(i, (i + by) % head_count) for i in range(head_count)]
         return lax.ppermute(value, "head", pairs)
 
+    kv = jnp.stack([key_states, value_states])
+    near = send(kv, along)
+    next_own = send(queries, down)
+    q_sibling = send(queries, sibling)
+    kv, q_sibling = lax.optimization_barrier((kv, q_sibling))
+    cross = send(kv, lambda i: along(sibling(i)))
+
     upto = jnp.arange(clip_lengths.shape[0])
     ends = jnp.sum(jnp.where(upto[None, :] <= upto[:, None], clip_lengths[None, :], 0), axis=1)
     owners = jnp.stack([me, me ^ 1, (me + ring) % ctx_count, ((me + ring) % ctx_count) ^ 1])
@@ -295,13 +302,6 @@
         jnp.where(ends[None, None, :] <= q_blocks[:, :, None], ends[None, None, :], 0), axis=-1
     )
     info = jnp.concatenate([bases, begin.reshape(-1)]).astype(jnp.int32)
-
-    kv = jnp.stack([key_states, value_states])
-    near = send(kv, along)
-    kv, info = lax.optimization_barrier((kv, info))
-    cross = send(kv, lambda i: along(sibling(i)))
-    next_own = send(queries, down)
-    q_sibling = send(queries, sibling)
 
     def base_of(step, of_core):
         chip = (place + jnp.where(core == 0, -step, step)) % RING_CHIPS

time: 90.3 us -> 92.7 us (1.027)
  the two profiles are of different devices: /device:TPU:128 before, /device:TPU:1 now
where the time goes in v2:
time: 92.7 us; the launch traced here: 92.6 us
  Pallas kernels  34.9 us (38%)
  starting transfers between devices  29.2 us (31%)
  waiting for transfers between devices  24.8 us (27%)
  other arithmetic  2.3 us (2%)
  local copies, waits for them, and re-layouts  1.06 us (1%)
    pallas_call x10, Pallas kernels, fold(): pl.pallas_call(functools.partial(fold_kernel, first, parts), out_shape=sh...  29.1 us
    ppermute x13, starting transfers between devices, send(): lax.ppermute(value, 'ctx', [(i, target(i)) for i in range(ctx_count)])  23.6 us
    ppermute x13, waiting for transfers between devices, send(): lax.ppermute(value, 'ctx', [(i, target(i)) for i in range(ctx_count)])  15.6 us
    ppermute x4, waiting for transfers between devices, turn(): return lax.ppermute(value, 'head', pairs)  9.16 us
    ppermute x4, starting transfers between devices, turn(): return lax.ppermute(value, 'head', pairs)  5.62 us
    pallas_call x1, Pallas kernels, project(): pl.pallas_call(project_kernel, grid=(steps,), out_shape=jax.ShapeDtypeStr...  3.66 us
    pallas_call x4, Pallas kernels, small_call(): pl.pallas_call(kernel, out_shape=out_shape, in_specs=[vmem_spec()] * len(...  2.12 us
  transfers between devices with their start and end apart: 17, of which 6 were waited for; matrix products, arithmetic and copies ran while one was open for 3% of the time, Pallas kernels for 28%

profile of v2, /device:TPU:1, one launch (start us, length us, event | category | flops | bytes accessed | tf_op | source)
XLA Modules:
  0.0 92.6 jit_solution(17787173033007420746)
XLA Ops:
  0.0 4.1 %collective-permute-start.2 = (bf16[1024,128]{1,0:T(8,128)(2,1)}, bf16[1024,128]{1,0:T(8,128)(2,1)S(1)}, u32[]{:S(2)}, u32[]{:S(2)}) collective-permute-start(bf16[1024,128]{1,0:T(8,128)(2,1)} %refs_0_.15), channel_id=1, source_target_pairs={{0,196},{4,192},{8,204},{12,200},{16,212},{20,208},{24,220},{28,21... | collective-permute-start | bytes 786440 | tf_op jit(solution)/shard_map/ppermute | solution.py:265
  4.1 0.5 collective-permute-start.1
  4.6 0.1 collective-permute-start
  4.7 1.1 %pad_maximum_fusion.refs_1_.refs_2_ = bf16[2,1024,128]{2,1,0:T(8,128)(2,1)S(1)} fusion(bf16[1,1024,128]{2,1,0:T(8,128)(2,1)} %bitcast.15, bf16[1,1024,128]{2,1,0:T(8,128)(2,1)} %bitcast.16), kind=kLoop, calls=%fused_computation | loop fusion | flops 262144 | bytes 1048576 | tf_op jit(solution)/shard_map/stack | solution.py:289
  5.8 5.7 %collective-permute-start.3 = (bf16[2,1024,128]{2,1,0:T(8,128)(2,1)S(1)}, bf16[2,1024,128]{2,1,0:T(8,128)(2,1)S(1)}, u32[]{:S(2)}, u32[]{:S(2)}) collective-permute-start(bf16[2,1024,128]{2,1,0:T(8,128)(2,1)S(1)} %pad_maximum_fusion.refs_1_.refs_2_), channel_id=1, source_target_pairs={{0,8},{4,60},{8,16},{12,4},{16,24},{20,12},{24,32},{28,20},{32,40}... | collective-permute-start | bytes 1572872 | tf_op jit(solution)/shard_map/ppermute | solution.py:265
  11.4 0.1 add_multiply_fusion
  11.5 0.1 iota_add_fusion
  11.6 0.0 collective-permute-done.refs_0_.refs_1_
  11.6 0.0 collective-permute-start.5
  11.6 0.8 select_reduce_fusion.1
  12.4 0.2 select_reduce_fusion
  12.8 0.1 reshape.86
  12.9 0.1 pad_add_fusion.info
  12.9 0.9 %copy-done.1 = bf16[1024,128]{1,0:T(8,128)(2,1)S(1)} copy-done((bf16[1024,128]{1,0:T(8,128)(2,1)S(1)}, bf16[1024,128]{1,0:T(8,128)(2,1)}, u32[]{:S(2)}) %copy-start.1) | copy-done | bytes 262168
  13.9 2.6 %fold.10 = (f32[4096,128]{1,0:T(8,128)S(1)}, f32[4096,256]{1,0:T(8,128)S(1)}) custom-call(s32[36]{0:T(128)S(1)} %pad_add_fusion.info, s32[1]{0:T(128)} %bitcast.8.key_base, bf16[1024,128]{1,0:T(8,128)(2,1)S(1)} %copy-done.1, bf16[2,1024,128]{2,1,0:T(8,128)(2,1)S(1)} %pad_maximum_fusion.refs_1_.refs_2_), custom_call_target="tpu_custom_call" | custom-call | flops 536870912 | bytes 1000000 | tf_op jit(solution)/shard_map/fold/pallas_call | solution.py:112
  16.5 0.6 fold.11
  17.0 4.6 %collective-permute-done.3.refs_4_ = bf16[2,1024,128]{2,1,0:T(8,128)(2,1)S(1)} collective-permute-done((bf16[2,1024,128]{2,1,0:T(8,128)(2,1)S(1)}, bf16[2,1024,128]{2,1,0:T(8,128)(2,1)S(1)}, u32[]{:S(2)}, u32[]{:S(2)}) %collective-permute-start.3) | collective-permute-done | bytes 524320 | tf_op jit(solution)/shard_map/ppermute | solution.py:265
  21.6 3.1 %collective-permute-start.4 = (bf16[2,1024,128]{2,1,0:T(8,128)(2,1)S(1)}, bf16[2,1024,128]{2,1,0:T(8,128)(2,1)S(1)}, u32[]{:S(2)}, u32[]{:S(2)}) collective-permute-start(bf16[2,1024,128]{2,1,0:T(8,128)(2,1)S(1)} %collective-permute-done.3.refs_4_), channel_id=1, source_target_pairs={{0,8},{4,60},{8,16},{12,4},{16,24},{20,12},{24,32},{28,20},{32,40}... | collective-permute-start | bytes 1572872 | tf_op jit(solution)/shard_map/ppermute | solution.py:265
  24.8 4.0 %fold.12 = (f32[4096,128]{1,0:T(8,128)S(1)}, f32[4096,256]{1,0:T(8,128)S(1)}) custom-call(s32[36]{0:T(128)S(1)} %pad_add_fusion.info, s32[1]{0:T(128)} %bitcast.10.key_base, bf16[1024,128]{1,0:T(8,128)(2,1)S(1)} %copy-done.1, bf16[1024,128]{1,0:T(8,128)(2,1)S(1)} %collective-permute-done.refs_0_.refs_1_, ...), custom_call_target="tpu_custom_call", output_to_operand_aliasing={{0}: (7, {}), {1}: (8, {})} | custom-call | flops 1073741824 | bytes 1000000 | tf_op jit(solution)/shard_map/fold/pallas_call | solution.py:112
  28.8 0.0 collective-permute-done.5.refs_4_
  28.8 0.1 collective-permute-start.7
  28.9 0.8 fold.13
  29.7 1.1 %collective-permute-done.4.refs_4_ = bf16[2,1024,128]{2,1,0:T(8,128)(2,1)S(1)} collective-permute-done((bf16[2,1024,128]{2,1,0:T(8,128)(2,1)S(1)}, bf16[2,1024,128]{2,1,0:T(8,128)(2,1)S(1)}, u32[]{:S(2)}, u32[]{:S(2)}) %collective-permute-start.4) | collective-permute-done | bytes 524320 | tf_op jit(solution)/shard_map/ppermute | solution.py:265
  30.9 3.1 %collective-permute-start.6 = (bf16[2,1024,128]{2,1,0:T(8,128)(2,1)S(1)}, bf16[2,1024,128]{2,1,0:T(8,128)(2,1)S(1)}, u32[]{:S(2)}, u32[]{:S(2)}) collective-permute-start(bf16[2,1024,128]{2,1,0:T(8,128)(2,1)S(1)} %collective-permute-done.4.refs_4_), channel_id=1, source_target_pairs={{0,8},{4,60},{8,16},{12,4},{16,24},{20,12},{24,32},{28,20},{32,40}... | collective-permute-start | bytes 1572872 | tf_op jit(solution)/shard_map/ppermute | solution.py:265
  34.0 4.1 %fold.14 = (f32[4096,128]{1,0:T(8,128)S(1)}, f32[4096,256]{1,0:T(8,128)S(1)}) custom-call(s32[36]{0:T(128)S(1)} %pad_add_fusion.info, s32[1]{0:T(128)} %bitcast.12.key_base, bf16[1024,128]{1,0:T(8,128)(2,1)S(1)} %copy-done.1, bf16[1024,128]{1,0:T(8,128)(2,1)S(1)} %collective-permute-done.refs_0_.refs_1_, ...), custom_call_target="tpu_custom_call", output_to_operand_aliasing={{0}: (7, {}), {1}: (8, {})} | custom-call | flops 6174015488 | bytes 1000000 | tf_op jit(solution)/shard_map/fold/pallas_call | solution.py:112
  38.1 1.5 %collective-permute-start.9 = (bf16[2,1024,128]{2,1,0:T(8,128)(2,1)S(1)}, bf16[2,1024,128]{2,1,0:T(8,128)(2,1)S(1)}, u32[]{:S(2)}, u32[]{:S(2)}) collective-permute-start(bf16[2,1024,128]{2,1,0:T(8,128)(2,1)S(1)} %collective-permute-done.7.refs_4_), channel_id=1, source_target_pairs={{0,8},{4,60},{8,16},{12,4},{16,24},{20,12},{24,32},{28,20},{32,40}... | collective-permute-start | bytes 1572872 | tf_op jit(solution)/shard_map/ppermute | solution.py:265
  39.6 4.1 %fold.15 = (f32[4096,128]{1,0:T(8,128)S(1)}, f32[4096,256]{1,0:T(8,128)S(1)}) custom-call(s32[36]{0:T(128)S(1)} %pad_add_fusion.info, s32[1]{0:T(128)} %bitcast.11.key_base, bf16[1024,128]{1,0:T(8,128)(2,1)S(1)} %copy-done.1, bf16[1024,128]{1,0:T(8,128)(2,1)S(1)} %collective-permute-done.refs_0_.refs_1_, ...), custom_call_target="tpu_custom_call", output_to_operand_aliasing={{0}: (7, {}), {1}: (8, {})} | custom-call | flops 6174015488 | bytes 1000000 | tf_op jit(solution)/shard_map/fold/pallas_call | solution.py:112
  43.7 1.5 %collective-permute-start.8 = (bf16[2,1024,128]{2,1,0:T(8,128)(2,1)S(1)}, bf16[2,1024,128]{2,1,0:T(8,128)(2,1)S(1)}, u32[]{:S(2)}, u32[]{:S(2)}) collective-permute-start(bf16[2,1024,128]{2,1,0:T(8,128)(2,1)S(1)} %collective-permute-done.6.refs_4_), channel_id=1, source_target_pairs={{0,8},{4,60},{8,16},{12,4},{16,24},{20,12},{24,32},{28,20},{32,40}... | collective-permute-start | bytes 1572872 | tf_op jit(solution)/shard_map/ppermute | solution.py:265
  45.2 4.0 %fold.16 = (f32[4096,128]{1,0:T(8,128)S(1)}, f32[4096,256]{1,0:T(8,128)S(1)}) custom-call(s32[36]{0:T(128)S(1)} %pad_add_fusion.info, s32[1]{0:T(128)} %bitcast.14.key_base, bf16[1024,128]{1,0:T(8,128)(2,1)S(1)} %copy-done.1, bf16[1024,128]{1,0:T(8,128)(2,1)S(1)} %collective-permute-done.refs_0_.refs_1_, ...), custom_call_target="tpu_custom_call", output_to_operand_aliasing={{0}: (7, {}), {1}: (8, {})} | custom-call | flops 6174015488 | bytes 1000000 | tf_op jit(solution)/shard_map/fold/pallas_call | solution.py:112
  49.3 4.1 %fold.17 = (f32[4096,128]{1,0:T(8,128)S(1)}, f32[4096,256]{1,0:T(8,128)S(1)}) custom-call(s32[36]{0:T(128)S(1)} %pad_add_fusion.info, s32[1]{0:T(128)} %bitcast.13.key_base, bf16[1024,128]{1,0:T(8,128)(2,1)S(1)} %copy-done.1, bf16[1024,128]{1,0:T(8,128)(2,1)S(1)} %collective-permute-done.refs_0_.refs_1_, ...), custom_call_target="tpu_custom_call", output_to_operand_aliasing={{0}: (7, {}), {1}: (8, {})} | custom-call | flops 6174015488 | bytes 1000000 | tf_op jit(solution)/shard_map/fold/pallas_call | solution.py:112
  53.4 0.8 fold.18
  54.2 4.1 %fold.19 = (f32[4096,128]{1,0:T(8,128)S(1)}, f32[4096,256]{1,0:T(8,128)S(1)}) custom-call(s32[36]{0:T(128)S(1)} %pad_add_fusion.info, s32[1]{0:T(128)} %bitcast.5.key_base, bf16[1024,128]{1,0:T(8,128)(2,1)S(1)} %copy-done.1, bf16[1024,128]{1,0:T(8,128)(2,1)S(1)} %collective-permute-done.refs_0_.refs_1_, ...), custom_call_target="tpu_custom_call", output_to_operand_aliasing={{0}: (7, {}), {1}: (8, {})} | custom-call | flops 6174015488 | bytes 1000000 | tf_op jit(solution)/shard_map/fold/pallas_call | solution.py:112
  58.3 0.2 leave_next.1
  58.5 3.6 %collective-permute-start.11 = (bf16[1072,128]{1,0:T(8,128)(2,1)S(1)}, bf16[1072,128]{1,0:T(8,128)(2,1)S(1)}, u32[]{:S(2)}, u32[]{:S(2)}) collective-permute-start(bf16[1072,128]{1,0:T(8,128)(2,1)S(1)} %leave_next.1), channel_id=1, source_target_pairs={{0,4},{4,0},{8,12},{12,8},{16,20},{20,16},{24,28},{28,24},{32,36},... | collective-permute-start | bytes 823304 | tf_op jit(solution)/shard_map/ppermute | solution.py:265
  62.1 0.2 leave_own.1
  62.3 0.1 collective-permute-start.10
  62.4 0.9 collective-permute-done.11.other
  63.3 0.7 pass_on.1
  64.0 0.0 copy-start
  64.0 0.1 collective-permute-start.12
  64.1 9.0 %collective-permute-done.12.back = bf16[1072,128]{1,0:T(8,128)(2,1)S(1)} collective-permute-done((bf16[1072,128]{1,0:T(8,128)(2,1)S(1)}, bf16[1072,128]{1,0:T(8,128)(2,1)S(1)}, u32[]{:S(2)}, u32[]{:S(2)}) %collective-permute-start.12) | collective-permute-done | bytes 274464 | tf_op jit(solution)/shard_map/ppermute | solution.py:265
  73.1 1.0 %join.1.own = bf16[1024,128]{1,0:T(8,128)(2,1)S(1)} custom-call(f32[4096,128]{1,0:T(8,128)S(1)} %get-tuple-element.67.m_ref, f32[4096,256]{1,0:T(8,128)S(1)} %get-tuple-element.68.a_ref, bf16[1072,128]{1,0:T(8,128)(2,1)S(1)} %collective-permute-done.10.other, bf16[1072,128]{1,0:T(8,128)(2,1)S(1)} %collective-permute-done.12.back), custom_call_target="tpu_custom_call" | custom-call | tf_op jit(solution)/shard_map/join/pallas_call | solution.py:201
  74.1 2.6 %collective-permute-start.14 = (bf16[1024,128]{1,0:T(8,128)(2,1)S(1)}, bf16[1024,128]{1,0:T(8,128)(2,1)S(1)}, u32[]{:S(2)}, u32[]{:S(2)}) collective-permute-start(bf16[1024,128]{1,0:T(8,128)(2,1)S(1)} %join.1.own), channel_id=1, source_target_pairs={{0,3},{1,0},{2,1},{3,2},{4,7},{5,4},{6,5},{7,6},{8,11},{9,8},{10,9... | collective-permute-start | bytes 786440 | tf_op jit(solution)/shard_map/ppermute | solution.py:287
  76.7 1.8 %collective-permute-start.16 = (bf16[512,128]{1,0:T(8,128)(2,1)S(1)}, bf16[512,128]{1,0:T(8,128)(2,1)S(1)}, u32[]{:S(2)}, u32[]{:S(2)}) collective-permute-start(bf16[512,128]{1,0:T(8,128)(2,1)S(1)} %get-tuple-element.69), channel_id=1, source_target_pairs={{0,2},{1,3},{2,0},{3,1},{4,6},{5,7},{6,4},{7,5},{8,10},{9,11},{10,... | collective-permute-start | bytes 393224 | tf_op jit(solution)/shard_map/ppermute | solution.py:287
  78.5 1.2 %collective-permute-start.15 = (bf16[512,128]{1,0:T(8,128)(2,1)S(1)}, bf16[512,128]{1,0:T(8,128)(2,1)S(1)}, u32[]{:S(2)}, u32[]{:S(2)}) collective-permute-start(bf16[512,128]{1,0:T(8,128)(2,1)S(1)} %get-tuple-element.70), channel_id=1, source_target_pairs={{0,2},{1,3},{2,0},{3,1},{4,6},{5,7},{6,4},{7,5},{8,10},{9,11},{10,... | collective-permute-start | bytes 393224 | tf_op jit(solution)/shard_map/ppermute | solution.py:287
  79.7 6.0 %collective-permute-done.16.far_b = bf16[512,128]{1,0:T(8,128)(2,1)S(1)} collective-permute-done((bf16[512,128]{1,0:T(8,128)(2,1)S(1)}, bf16[512,128]{1,0:T(8,128)(2,1)S(1)}, u32[]{:S(2)}, u32[]{:S(2)}) %collective-permute-start.16) | collective-permute-done | bytes 131104 | tf_op jit(solution)/shard_map/ppermute | solution.py:287
  85.7 3.1 %collective-permute-done.15.far_a = bf16[512,128]{1,0:T(8,128)(2,1)S(1)} collective-permute-done((bf16[512,128]{1,0:T(8,128)(2,1)S(1)}, bf16[512,128]{1,0:T(8,128)(2,1)S(1)}, u32[]{:S(2)}, u32[]{:S(2)}) %collective-permute-start.15) | collective-permute-done | bytes 131104 | tf_op jit(solution)/shard_map/ppermute | solution.py:287
  88.9 3.7 %project.1 = bf16[1024,1536]{1,0:T(8,128)(2,1)} custom-call(s32[1]{0:T(128)} %bitcast.heads, bf16[1024,128]{1,0:T(8,128)(2,1)S(1)} %join.1.own, bf16[1024,128]{1,0:T(8,128)(2,1)S(1)} %collective-permute-done.13.left, bf16[1024,128]{1,0:T(8,128)(2,1)S(1)} %collective-permute-done.14.right, bf16[512,128]{1,0:T(8,128)(2,1)S(1)} %collective-permute-done.15.far_a, ...), custom_call_target="tpu_custom_call" | custom-call | tf_op jit(solution)/shard_map/project/pallas_call | solution.py:240
  (13 shorter events, 0.0 us)
Async XLA Ops:
  0.0 24.8 %collective-permute-start.2 = (bf16[1024,128]{1,0:T(8,128)(2,1)}, bf16[1024,128]{1,0:T(8,128)(2,1)S(1)}, u32[]{:S(2)}, u32[]{:S(2)}) collective-permute-start(bf16[1024,128]{1,0:T(8,128)(2,1)} %refs_0_.15), channel_id=1, source_target_pairs={{0,196},{4,192},{8,204},{12,200},{16,212},{20,208},{24,220},{28,21... | collective-permute-start | bytes 786440 | tf_op jit(solution)/shard_map/ppermute | solution.py:265
  4.1 20.6 %collective-permute-start.1 = (bf16[1024,128]{1,0:T(8,128)(2,1)}, bf16[1024,128]{1,0:T(8,128)(2,1)S(1)}, u32[]{:S(2)}, u32[]{:S(2)}) collective-permute-start(bf16[1024,128]{1,0:T(8,128)(2,1)} %refs_0_.15), channel_id=1, source_target_pairs={{0,192},{4,196},{8,200},{12,204},{16,208},{20,212},{24,216},{28,22... | collective-permute-start | bytes 786440 | tf_op jit(solution)/shard_map/ppermute | solution.py:265
  4.6 7.0 %collective-permute-start = (bf16[1024,128]{1,0:T(8,128)(2,1)}, bf16[1024,128]{1,0:T(8,128)(2,1)S(1)}, u32[]{:S(2)}, u32[]{:S(2)}) collective-permute-start(bf16[1024,128]{1,0:T(8,128)(2,1)} %refs_0_.15), channel_id=1, source_target_pairs={{0,4},{4,0},{8,12},{12,8},{16,20},{20,16},{24,28},{28,24},{32,36},... | collective-permute-start | bytes 786440 | tf_op jit(solution)/shard_map/ppermute | solution.py:265
  5.8 15.8 %collective-permute-start.3 = (bf16[2,1024,128]{2,1,0:T(8,128)(2,1)S(1)}, bf16[2,1024,128]{2,1,0:T(8,128)(2,1)S(1)}, u32[]{:S(2)}, u32[]{:S(2)}) collective-permute-start(bf16[2,1024,128]{2,1,0:T(8,128)(2,1)S(1)} %pad_maximum_fusion.refs_1_.refs_2_), channel_id=1, source_target_pairs={{0,8},{4,60},{8,16},{12,4},{16,24},{20,12},{24,32},{28,20},{32,40}... | collective-permute-start | bytes 1572872 | tf_op jit(solution)/shard_map/ppermute | solution.py:265
  11.6 17.2 %collective-permute-start.5 = (bf16[2,1024,128]{2,1,0:T(8,128)(2,1)S(1)}, bf16[2,1024,128]{2,1,0:T(8,128)(2,1)S(1)}, u32[]{:S(2)}, u32[]{:S(2)}) collective-permute-start(bf16[2,1024,128]{2,1,0:T(8,128)(2,1)S(1)} %pad_maximum_fusion.refs_1_.refs_2_), channel_id=1, source_target_pairs={{0,60},{4,8},{8,4},{12,16},{16,12},{20,24},{24,20},{28,32},{32,28}... | collective-permute-start | bytes 1572872 | tf_op jit(solution)/shard_map/ppermute | solution.py:265
  12.9 1.0 %copy-start.1 = (bf16[1024,128]{1,0:T(8,128)(2,1)S(1)}, bf16[1024,128]{1,0:T(8,128)(2,1)}, u32[]{:S(2)}) copy-start(bf16[1024,128]{1,0:T(8,128)(2,1)} %refs_0_.15) | copy-start | bytes 786436
  21.6 9.2 %collective-permute-start.4 = (bf16[2,1024,128]{2,1,0:T(8,128)(2,1)S(1)}, bf16[2,1024,128]{2,1,0:T(8,128)(2,1)S(1)}, u32[]{:S(2)}, u32[]{:S(2)}) collective-permute-start(bf16[2,1024,128]{2,1,0:T(8,128)(2,1)S(1)} %collective-permute-done.3.refs_4_), channel_id=1, source_target_pairs={{0,8},{4,60},{8,16},{12,4},{16,24},{20,12},{24,32},{28,20},{32,40}... | collective-permute-start | bytes 1572872 | tf_op jit(solution)/shard_map/ppermute | solution.py:265
  28.8 9.2 %collective-permute-start.7 = (bf16[2,1024,128]{2,1,0:T(8,128)(2,1)S(1)}, bf16[2,1024,128]{2,1,0:T(8,128)(2,1)S(1)}, u32[]{:S(2)}, u32[]{:S(2)}) collective-permute-start(bf16[2,1024,128]{2,1,0:T(8,128)(2,1)S(1)} %collective-permute-done.5.refs_4_), channel_id=1, source_target_pairs={{0,8},{4,60},{8,16},{12,4},{16,24},{20,12},{24,32},{28,20},{32,40}... | collective-permute-start | bytes 1572872 | tf_op jit(solution)/shard_map/ppermute | solution.py:265
  30.9 12.8 %collective-permute-start.6 = (bf16[2,1024,128]{2,1,0:T(8,128)(2,1)S(1)}, bf16[2,1024,128]{2,1,0:T(8,128)(2,1)S(1)}, u32[]{:S(2)}, u32[]{:S(2)}) collective-permute-start(bf16[2,1024,128]{2,1,0:T(8,128)(2,1)S(1)} %collective-permute-done.4.refs_4_), channel_id=1, source_target_pairs={{0,8},{4,60},{8,16},{12,4},{16,24},{20,12},{24,32},{28,20},{32,40}... | collective-permute-start | bytes 1572872 | tf_op jit(solution)/shard_map/ppermute | solution.py:265
  38.1 11.2 %collective-permute-start.9 = (bf16[2,1024,128]{2,1,0:T(8,128)(2,1)S(1)}, bf16[2,1024,128]{2,1,0:T(8,128)(2,1)S(1)}, u32[]{:S(2)}, u32[]{:S(2)}) collective-permute-start(bf16[2,1024,128]{2,1,0:T(8,128)(2,1)S(1)} %collective-permute-done.7.refs_4_), channel_id=1, source_target_pairs={{0,8},{4,60},{8,16},{12,4},{16,24},{20,12},{24,32},{28,20},{32,40}... | collective-permute-start | bytes 1572872 | tf_op jit(solution)/shard_map/ppermute | solution.py:265
  43.7 10.5 %collective-permute-start.8 = (bf16[2,1024,128]{2,1,0:T(8,128)(2,1)S(1)}, bf16[2,1024,128]{2,1,0:T(8,128)(2,1)S(1)}, u32[]{:S(2)}, u32[]{:S(2)}) collective-permute-start(bf16[2,1024,128]{2,1,0:T(8,128)(2,1)S(1)} %collective-permute-done.6.refs_4_), channel_id=1, source_target_pairs={{0,8},{4,60},{8,16},{12,4},{16,24},{20,12},{24,32},{28,20},{32,40}... | collective-permute-start | bytes 1572872 | tf_op jit(solution)/shard_map/ppermute | solution.py:265
  58.5 4.8 %collective-permute-start.11 = (bf16[1072,128]{1,0:T(8,128)(2,1)S(1)}, bf16[1072,128]{1,0:T(8,128)(2,1)S(1)}, u32[]{:S(2)}, u32[]{:S(2)}) collective-permute-start(bf16[1072,128]{1,0:T(8,128)(2,1)S(1)} %leave_next.1), channel_id=1, source_target_pairs={{0,4},{4,0},{8,12},{12,8},{16,20},{20,16},{24,28},{28,24},{32,36},... | collective-permute-start | bytes 823304 | tf_op jit(solution)/shard_map/ppermute | solution.py:265
  62.3 1.8 %collective-permute-start.10 = (bf16[1072,128]{1,0:T(8,128)(2,1)S(1)}, bf16[1072,128]{1,0:T(8,128)(2,1)S(1)}, u32[]{:S(2)}, u32[]{:S(2)}) collective-permute-start(bf16[1072,128]{1,0:T(8,128)(2,1)S(1)} %leave_own.1), channel_id=1, source_target_pairs={{0,4},{4,0},{8,12},{12,8},{16,20},{20,16},{24,28},{28,24},{32,36},... | collective-permute-start | bytes 823304 | tf_op jit(solution)/shard_map/ppermute | solution.py:265
  64.0 24.9 %copy-start = (bf16[512,1536]{1,0:T(8,128)(2,1)S(1)}, bf16[512,1536]{1,0:T(8,128)(2,1)}, u32[]{:S(2)}) copy-start(bf16[512,1536]{1,0:T(8,128)(2,1)} %weight.1) | copy-start | bytes 4718596
  64.0 9.1 %collective-permute-start.12 = (bf16[1072,128]{1,0:T(8,128)(2,1)S(1)}, bf16[1072,128]{1,0:T(8,128)(2,1)S(1)}, u32[]{:S(2)}, u32[]{:S(2)}) collective-permute-start(bf16[1072,128]{1,0:T(8,128)(2,1)S(1)} %pass_on.1), channel_id=1, source_target_pairs={{0,64},{4,68},{8,72},{12,76},{16,80},{20,84},{24,88},{28,92},{32,9... | collective-permute-start | bytes 823304 | tf_op jit(solution)/shard_map/ppermute | solution.py:265
  74.1 14.8 %collective-permute-start.14 = (bf16[1024,128]{1,0:T(8,128)(2,1)S(1)}, bf16[1024,128]{1,0:T(8,128)(2,1)S(1)}, u32[]{:S(2)}, u32[]{:S(2)}) collective-permute-start(bf16[1024,128]{1,0:T(8,128)(2,1)S(1)} %join.1.own), channel_id=1, source_target_pairs={{0,3},{1,0},{2,1},{3,2},{4,7},{5,4},{6,5},{7,6},{8,11},{9,8},{10,9... | collective-permute-start | bytes 786440 | tf_op jit(solution)/shard_map/ppermute | solution.py:287
  76.6 12.2 %collective-permute-start.13 = (bf16[1024,128]{1,0:T(8,128)(2,1)S(1)}, bf16[1024,128]{1,0:T(8,128)(2,1)S(1)}, u32[]{:S(2)}, u32[]{:S(2)}) collective-permute-start(bf16[1024,128]{1,0:T(8,128)(2,1)S(1)} %join.1.own), channel_id=1, source_target_pairs={{0,1},{1,2},{2,3},{3,0},{4,5},{5,6},{6,7},{7,4},{8,9},{9,10},{10,1... | collective-permute-start | bytes 786440 | tf_op jit(solution)/shard_map/ppermute | solution.py:287
  76.7 9.1 %collective-permute-start.16 = (bf16[512,128]{1,0:T(8,128)(2,1)S(1)}, bf16[512,128]{1,0:T(8,128)(2,1)S(1)}, u32[]{:S(2)}, u32[]{:S(2)}) collective-permute-start(bf16[512,128]{1,0:T(8,128)(2,1)S(1)} %get-tuple-element.69), channel_id=1, source_target_pairs={{0,2},{1,3},{2,0},{3,1},{4,6},{5,7},{6,4},{7,5},{8,10},{9,11},{10,... | collective-permute-start | bytes 393224 | tf_op jit(solution)/shard_map/ppermute | solution.py:287
  78.5 10.4 %collective-permute-start.15 = (bf16[512,128]{1,0:T(8,128)(2,1)S(1)}, bf16[512,128]{1,0:T(8,128)(2,1)S(1)}, u32[]{:S(2)}, u32[]{:S(2)}) collective-permute-start(bf16[512,128]{1,0:T(8,128)(2,1)S(1)} %get-tuple-element.70), channel_id=1, source_target_pairs={{0,2},{1,3},{2,0},{3,1},{4,6},{5,7},{6,4},{7,5},{8,10},{9,11},{10,... | collective-permute-start | bytes 393224 | tf_op jit(solution)/shard_map/ppermute | solution.py:287

commit v3 on v1

--- a/solution.py
+++ b/solution.py
@@ -132,6 +132,9 @@
     return row == lax.broadcasted_iota(jnp.int32, (BLOCK, BLOCK), 1)
 
 
+PIECE_ROWS = 16
+
+
 def pack(out_ref, out, log_sum):
     tok = out.shape[0]
     blocks = tok // BLOCK
@@ -140,29 +143,29 @@
         jnp.sum(jnp.where(on, log_sum[i * BLOCK : (i + 1) * BLOCK, :], 0.0), axis=0, keepdims=True)
         for i in range(blocks)
     ]
+    rows.append(jnp.zeros((PIECE_ROWS - blocks, BLOCK), jnp.float32))
     rest = jnp.concatenate(rows, axis=0)
     out_ref[:tok, :] = out.astype(jnp.bfloat16)
     for k in range(3):
         piece = rest.astype(jnp.bfloat16)
         rest = rest - piece.astype(jnp.float32)
-        both = jnp.concatenate([piece.astype(jnp.float32), jnp.zeros((blocks, BLOCK), jnp.float32)])
-        out_ref[tok + 2 * blocks * k : tok + 2 * blocks * (k + 1), :] = both.astype(jnp.bfloat16)
-
-
-def unpack(ref, tok):
-    blocks = tok // BLOCK
+        out_ref[tok + PIECE_ROWS * k : tok + PIECE_ROWS * (k + 1), :] = piece
+
+
+def unpack(ref, rows):
     on = diagonal()
+    tok = ref.shape[0] - 3 * PIECE_ROWS
     tail = ref[tok:, :].astype(jnp.float32)
-    log_rows = sum(tail[2 * blocks * k : 2 * blocks * k + blocks, :] for k in range(3))
+    log_rows = sum(tail[PIECE_ROWS * k : PIECE_ROWS * (k + 1), :] for k in range(3))
     columns = [
         jnp.sum(jnp.where(on, log_rows[i : i + 1, :], 0.0), axis=1, keepdims=True)
-        for i in range(blocks)
+        for i in range(rows.start // BLOCK, rows.stop // BLOCK)
     ]
-    return ref[:tok, :].astype(jnp.float32), jnp.concatenate(columns, axis=0)
+    return ref[rows, :].astype(jnp.float32), jnp.concatenate(columns, axis=0)
 
 
 def packed_shape(tok):
-    return jax.ShapeDtypeStruct((tok + 6 * (tok // BLOCK), HEAD_DIM), jnp.bfloat16)
+    return jax.ShapeDtypeStruct((tok + 3 * PIECE_ROWS, HEAD_DIM), jnp.bfloat16)
 
 
 def own_part(m_ref, a_ref, rows):
@@ -186,14 +189,14 @@
     pack_state(out_ref, *own_part(m_ref, a_ref, slice(part * tok, (part + 1) * tok)))
 
 
-def pass_on_kernel(tok, part, m_ref, a_ref, other, out_ref):
-    state = own_part(m_ref, a_ref, slice(part * tok, (part + 1) * tok))
-    pack_state(out_ref, *mix(*state, *unpack(other, tok)))
-
-
-def join_kernel(tok, m_ref, a_ref, other, back, out_ref):
-    state = mix(*own_part(m_ref, a_ref, slice(0, tok)), *unpack(other, tok))
-    _, num, den = mix(*state, *unpack(back, tok))
+def pass_on_kernel(tok, part, rows, m_ref, a_ref, other, out_ref):
+    state = own_part(m_ref, a_ref, slice(part * tok + rows.start, part * tok + rows.stop))
+    pack_state(out_ref, *mix(*state, *unpack(other, rows)))
+
+
+def join_kernel(rows, m_ref, a_ref, other, back, out_ref):
+    state = mix(*own_part(m_ref, a_ref, rows), *unpack(other, rows))
+    _, num, den = mix(*state, *unpack(back, slice(0, rows.stop - rows.start)))
     out_ref[...] = (num / den).astype(jnp.bfloat16)
 
 
@@ -208,7 +211,8 @@
     )(*args)
 
 
-def project_kernel(heads, own, left, right, far_a, far_b, weight, out_ref, lhs):
+def project_kernel(heads, own, left, right, far, weight, *refs):
+    out_ref, lhs = refs[-2:]
     step = pl.program_id(0)
     h = heads[0]
     count = weight.shape[0] // HEAD_DIM
@@ -216,16 +220,9 @@
 
     @pl.when(step == 0)
     def _():
-        half = far_a.shape[0]
-        for by, piece, rows in (
-            (0, own, slice(0, 2 * half)),
-            (count - 1, left, slice(0, 2 * half)),
-            (1, right, slice(0, 2 * half)),
-            (2, far_a, slice(0, half)),
-            (2, far_b, slice(half, 2 * half)),
-        ):
+        for by, piece in ((0, own), (count - 1, left), (1, right), (2, far)):
             column = pl.multiple_of(lax.rem(h + by, count) * HEAD_DIM, HEAD_DIM)
-            lhs[rows, pl.ds(column, HEAD_DIM)] = piece[...]
+            lhs[:, pl.ds(column, HEAD_DIM)] = piece[...]
 
     columns = pl.ds(pl.multiple_of(step * width, width), width)
     out_ref[...] = jnp.dot(
@@ -233,20 +230,29 @@
     ).astype(jnp.bfloat16)
 
 
-def project(heads, pieces, weight):
-    tok = pieces[0].shape[0]
+def project(heads, pieces, weight, tok, before):
+    rows = pieces[0].shape[0]
     steps = 3
     width = weight.shape[1] // steps
+    row_block = 0 if before is None else 1
     return pl.pallas_call(
         project_kernel,
         grid=(steps,),
         out_shape=jax.ShapeDtypeStruct((tok, weight.shape[1]), jnp.bfloat16),
-        in_specs=[smem_spec()] + [vmem_spec()] * 6,
-        out_specs=pl.BlockSpec((tok, width), lambda i: (0, i)),
-        scratch_shapes=[pltpu.VMEM((tok, weight.shape[0]), jnp.bfloat16)],
+        in_specs=[smem_spec()]
+        + [vmem_spec()] * 5
+        + ([] if before is None else [pl.BlockSpec(memory_space=pl.ANY)]),
+        out_specs=pl.BlockSpec((rows, width), lambda i: (row_block, i)),
+        scratch_shapes=[pltpu.VMEM((rows, weight.shape[0]), jnp.bfloat16)],
+        input_output_aliases={} if before is None else {6: 0},
         compiler_params=pltpu.CompilerParams(vmem_limit_bytes=VMEM_LIMIT),
+        cost_estimate=pl.CostEstimate(
+            flops=2 * rows * weight.shape[0] * weight.shape[1],
+            bytes_accessed=2 * rows * weight.shape[1],
+            transcendentals=0,
+        ),
         name="project",
-    )(heads, *pieces, weight)
+    )(heads, *pieces, weight, *([] if before is None else [before]))
 
 
 def shards(queries, key_states, value_states, clip_lengths, out_weight):
@@ -329,30 +335,45 @@
         )
 
     packed = packed_shape(tok)
+    half = tok // 2
+    halves = (slice(0, half), slice(half, tok))
     leave = functools.partial(leave_kernel, tok)
     next_there = send(small_call(functools.partial(leave, 3), "leave_next", packed, *state), sibling)
     own_there = send(small_call(functools.partial(leave, 1), "leave_own", packed, *state), sibling)
-    passed = small_call(
-        functools.partial(pass_on_kernel, tok, 2), "pass_on", packed, *state, next_there
-    )
-    back = send(passed, up)
-    attended = small_call(
-        functools.partial(join_kernel, tok),
-        "join",
-        jax.ShapeDtypeStruct((tok, HEAD_DIM), jnp.bfloat16),
-        *state,
-        own_there,
-        back,
-    )
-    half = tok // 2
-    pieces = (
-        attended,
-        turn(attended, 1),
-        turn(attended, -1),
-        turn(attended[:half], 2),
-        turn(attended[half:], -2),
-    )
-    return project(head.reshape(1).astype(jnp.int32), pieces, out_weight)
+    back = [
+        send(
+            small_call(
+                functools.partial(pass_on_kernel, tok, 2, rows),
+                "pass_on",
+                packed_shape(half),
+                *state,
+                next_there,
+            ),
+            up,
+        )
+        for rows in halves
+    ]
+    pieces = []
+    for rows, returned in zip(halves, back):
+        attended = small_call(
+            functools.partial(join_kernel, rows),
+            "join",
+            jax.ShapeDtypeStruct((half, HEAD_DIM), jnp.bfloat16),
+            *state,
+            own_there,
+            returned,
+        )
+        pieces.append(
+            (
+                attended,
+                turn(attended, 1),
+                turn(attended, -1),
+                turn(attended, 2),
+            )
+        )
+    heads = head.reshape(1).astype(jnp.int32)
+    first = project(heads, pieces[0], out_weight, tok, None)
+    return project(heads, pieces[1], out_weight, tok, first)
 
 
 def solution(mesh):

time: 90.3 us -> 86.6 us (0.959)
  the two profiles are of different devices: /device:TPU:128 before, /device:TPU:1 now
where the time goes in v3:
time: 86.6 us; the launch traced here: 87.7 us
  starting transfers between devices  34.8 us (40%)
  Pallas kernels  26.3 us (30%)
  waiting for transfers between devices  23.1 us (27%)
  other arithmetic  2.3 us (3%)
  local copies, waits for them, and re-layouts  1.07 us (1%)
    ppermute x14, starting transfers between devices, send(): lax.ppermute(value, 'ctx', [(i, target(i)) for i in range(ctx_count)])  27.7 us
    pallas_call x10, Pallas kernels, fold(): pl.pallas_call(functools.partial(fold_kernel, first, parts), out_shape=sh...  18.9 us
    ppermute x14, waiting for transfers between devices, send(): lax.ppermute(value, 'ctx', [(i, target(i)) for i in range(ctx_count)])  17.6 us
    ppermute x6, starting transfers between devices, turn(): return lax.ppermute(value, 'head', pairs)  7.09 us
    ppermute x6, waiting for transfers between devices, turn(): return lax.ppermute(value, 'head', pairs)  5.44 us
    pallas_call x2, Pallas kernels, project(): pl.pallas_call(project_kernel, grid=(steps,), out_shape=jax.ShapeDtypeStr...  5.21 us
    pallas_call x6, Pallas kernels, small_call(): pl.pallas_call(kernel, out_shape=out_shape, in_specs=[vmem_spec()] * len(...  2.26 us
  transfers between devices with their start and end apart: 20, of which 9 were waited for; matrix products, arithmetic and copies ran while one was open for 1% of the time, Pallas kernels for 22%

profile of v3, /device:TPU:1, one launch (start us, length us, event | category | flops | bytes accessed | tf_op | source)
XLA Modules:
  0.0 87.7 jit_solution(4355934417676612832)
XLA Ops:
  0.0 1.1 %pad_maximum_fusion.refs_1_.refs_2_ = bf16[2,1024,128]{2,1,0:T(8,128)(2,1)S(1)} fusion(bf16[1,1024,128]{2,1,0:T(8,128)(2,1)} %bitcast.15, bf16[1,1024,128]{2,1,0:T(8,128)(2,1)} %bitcast.16), kind=kLoop, calls=%fused_computation | loop fusion | flops 262144 | bytes 1048576 | tf_op jit(solution)/shard_map/stack | solution.py:305
  1.1 6.5 %collective-permute-start.3 = (bf16[2,1024,128]{2,1,0:T(8,128)(2,1)S(1)}, bf16[2,1024,128]{2,1,0:T(8,128)(2,1)S(1)}, u32[]{:S(2)}, u32[]{:S(2)}) collective-permute-start(bf16[2,1024,128]{2,1,0:T(8,128)(2,1)S(1)} %pad_maximum_fusion.refs_1_.refs_2_), channel_id=1, source_target_pairs={{0,8},{4,60},{8,16},{12,4},{16,24},{20,12},{24,32},{28,20},{32,40}... | collective-permute-start | bytes 1572872 | tf_op jit(solution)/shard_map/ppermute | solution.py:271
  7.6 0.8 select_reduce_fusion.1
  8.5 0.2 select_reduce_fusion
  8.9 1.1 %collective-permute-start = (bf16[1024,128]{1,0:T(8,128)(2,1)}, bf16[1024,128]{1,0:T(8,128)(2,1)S(1)}, u32[]{:S(2)}, u32[]{:S(2)}) collective-permute-start(bf16[1024,128]{1,0:T(8,128)(2,1)} %refs_0_.15), channel_id=1, source_target_pairs={{0,4},{4,0},{8,12},{12,8},{16,20},{20,16},{24,28},{28,24},{32,36},... | collective-permute-start | bytes 786440 | tf_op jit(solution)/shard_map/ppermute | solution.py:271
  10.0 2.6 %collective-permute-start.2 = (bf16[1024,128]{1,0:T(8,128)(2,1)}, bf16[1024,128]{1,0:T(8,128)(2,1)S(1)}, u32[]{:S(2)}, u32[]{:S(2)}) collective-permute-start(bf16[1024,128]{1,0:T(8,128)(2,1)} %refs_0_.15), channel_id=1, source_target_pairs={{0,196},{4,192},{8,204},{12,200},{16,212},{20,208},{24,220},{28,21... | collective-permute-start | bytes 786440 | tf_op jit(solution)/shard_map/ppermute | solution.py:271
  12.6 0.5 collective-permute-start.1
  13.1 1.0 %copy-done.1 = bf16[1024,128]{1,0:T(8,128)(2,1)S(1)} copy-done((bf16[1024,128]{1,0:T(8,128)(2,1)S(1)}, bf16[1024,128]{1,0:T(8,128)(2,1)}, u32[]{:S(2)}) %copy-start.1) | copy-done | bytes 262168
  14.1 2.6 %fold.10 = (f32[4096,128]{1,0:T(8,128)S(1)}, f32[4096,256]{1,0:T(8,128)S(1)}) custom-call(s32[36]{0:T(128)S(1)} %pad_add_fusion.info, s32[1]{0:T(128)} %bitcast.8.key_base, bf16[1024,128]{1,0:T(8,128)(2,1)S(1)} %copy-done.1, bf16[2,1024,128]{2,1,0:T(8,128)(2,1)S(1)} %pad_maximum_fusion.refs_1_.refs_2_), custom_call_target="tpu_custom_call" | custom-call | flops 536870912 | bytes 1000000 | tf_op jit(solution)/shard_map/fold/pallas_call | solution.py:112
  16.7 0.6 fold.11
  17.2 2.5 %collective-permute-start.4 = (bf16[2,1024,128]{2,1,0:T(8,128)(2,1)S(1)}, bf16[2,1024,128]{2,1,0:T(8,128)(2,1)S(1)}, u32[]{:S(2)}, u32[]{:S(2)}) collective-permute-start(bf16[2,1024,128]{2,1,0:T(8,128)(2,1)S(1)} %collective-permute-done.3.refs_4_), channel_id=1, source_target_pairs={{0,8},{4,60},{8,16},{12,4},{16,24},{20,12},{24,32},{28,20},{32,40}... | collective-permute-start | bytes 1572872 | tf_op jit(solution)/shard_map/ppermute | solution.py:271
  19.7 4.3 %collective-permute-done.1.refs_2_.refs_0_ = bf16[1024,128]{1,0:T(8,128)(2,1)S(1)} collective-permute-done((bf16[1024,128]{1,0:T(8,128)(2,1)}, bf16[1024,128]{1,0:T(8,128)(2,1)S(1)}, u32[]{:S(2)}, u32[]{:S(2)}) %collective-permute-start.1) | collective-permute-done | bytes 262176 | tf_op jit(solution)/shard_map/ppermute | solution.py:271
  24.1 0.6 fold.12
  24.7 0.8 collective-permute-start.7
  25.5 0.8 fold.13
  26.4 2.6 %collective-permute-start.6 = (bf16[2,1024,128]{2,1,0:T(8,128)(2,1)S(1)}, bf16[2,1024,128]{2,1,0:T(8,128)(2,1)S(1)}, u32[]{:S(2)}, u32[]{:S(2)}) collective-permute-start(bf16[2,1024,128]{2,1,0:T(8,128)(2,1)S(1)} %collective-permute-done.4.refs_4_), channel_id=1, source_target_pairs={{0,8},{4,60},{8,16},{12,4},{16,24},{20,12},{24,32},{28,20},{32,40}... | collective-permute-start | bytes 1572872 | tf_op jit(solution)/shard_map/ppermute | solution.py:271
  29.0 0.6 fold.14
  29.6 3.2 %collective-permute-done.7.refs_4_ = bf16[2,1024,128]{2,1,0:T(8,128)(2,1)S(1)} collective-permute-done((bf16[2,1024,128]{2,1,0:T(8,128)(2,1)S(1)}, bf16[2,1024,128]{2,1,0:T(8,128)(2,1)S(1)}, u32[]{:S(2)}, u32[]{:S(2)}) %collective-permute-start.7) | collective-permute-done | bytes 524320 | tf_op jit(solution)/shard_map/ppermute | solution.py:271
  32.8 1.9 %collective-permute-start.9 = (bf16[2,1024,128]{2,1,0:T(8,128)(2,1)S(1)}, bf16[2,1024,128]{2,1,0:T(8,128)(2,1)S(1)}, u32[]{:S(2)}, u32[]{:S(2)}) collective-permute-start(bf16[2,1024,128]{2,1,0:T(8,128)(2,1)S(1)} %collective-permute-done.7.refs_4_), channel_id=1, source_target_pairs={{0,8},{4,60},{8,16},{12,4},{16,24},{20,12},{24,32},{28,20},{32,40}... | collective-permute-start | bytes 1572872 | tf_op jit(solution)/shard_map/ppermute | solution.py:271
  34.8 0.6 fold.15
  35.4 3.3 %collective-permute-done.6.refs_4_ = bf16[2,1024,128]{2,1,0:T(8,128)(2,1)S(1)} collective-permute-done((bf16[2,1024,128]{2,1,0:T(8,128)(2,1)S(1)}, bf16[2,1024,128]{2,1,0:T(8,128)(2,1)S(1)}, u32[]{:S(2)}, u32[]{:S(2)}) %collective-permute-start.6) | collective-permute-done | bytes 524320 | tf_op jit(solution)/shard_map/ppermute | solution.py:271
  38.7 1.6 %collective-permute-start.8 = (bf16[2,1024,128]{2,1,0:T(8,128)(2,1)S(1)}, bf16[2,1024,128]{2,1,0:T(8,128)(2,1)S(1)}, u32[]{:S(2)}, u32[]{:S(2)}) collective-permute-start(bf16[2,1024,128]{2,1,0:T(8,128)(2,1)S(1)} %collective-permute-done.6.refs_4_), channel_id=1, source_target_pairs={{0,8},{4,60},{8,16},{12,4},{16,24},{20,12},{24,32},{28,20},{32,40}... | collective-permute-start | bytes 1572872 | tf_op jit(solution)/shard_map/ppermute | solution.py:271
  40.4 4.0 %fold.16 = (f32[4096,128]{1,0:T(8,128)S(1)}, f32[4096,256]{1,0:T(8,128)S(1)}) custom-call(s32[36]{0:T(128)S(1)} %pad_add_fusion.info, s32[1]{0:T(128)} %bitcast.14.key_base, bf16[1024,128]{1,0:T(8,128)(2,1)S(1)} %copy-done.1, bf16[1024,128]{1,0:T(8,128)(2,1)S(1)} %collective-permute-done.refs_0_.refs_1_, ...), custom_call_target="tpu_custom_call", output_to_operand_aliasing={{0}: (7, {}), {1}: (8, {})} | custom-call | flops 6174015488 | bytes 1000000 | tf_op jit(solution)/shard_map/fold/pallas_call | solution.py:112
  44.4 4.1 %fold.17 = (f32[4096,128]{1,0:T(8,128)S(1)}, f32[4096,256]{1,0:T(8,128)S(1)}) custom-call(s32[36]{0:T(128)S(1)} %pad_add_fusion.info, s32[1]{0:T(128)} %bitcast.13.key_base, bf16[1024,128]{1,0:T(8,128)(2,1)S(1)} %copy-done.1, bf16[1024,128]{1,0:T(8,128)(2,1)S(1)} %collective-permute-done.refs_0_.refs_1_, ...), custom_call_target="tpu_custom_call", output_to_operand_aliasing={{0}: (7, {}), {1}: (8, {})} | custom-call | flops 6174015488 | bytes 1000000 | tf_op jit(solution)/shard_map/fold/pallas_call | solution.py:112
  48.5 0.8 fold.18
  49.3 0.6 collective-permute-done.8.refs_4_
  50.0 4.1 %fold.19 = (f32[4096,128]{1,0:T(8,128)S(1)}, f32[4096,256]{1,0:T(8,128)S(1)}) custom-call(s32[36]{0:T(128)S(1)} %pad_add_fusion.info, s32[1]{0:T(128)} %bitcast.7.key_base, bf16[1024,128]{1,0:T(8,128)(2,1)S(1)} %copy-done.1, bf16[1024,128]{1,0:T(8,128)(2,1)S(1)} %collective-permute-done.refs_0_.refs_1_, ...), custom_call_target="tpu_custom_call", output_to_operand_aliasing={{0}: (7, {}), {1}: (8, {})} | custom-call | flops 6174015488 | bytes 1000000 | tf_op jit(solution)/shard_map/fold/pallas_call | solution.py:112
  54.0 0.2 leave_next.1
  54.2 6.8 %collective-permute-start.11 = (bf16[1072,128]{1,0:T(8,128)(2,1)S(1)}, bf16[1072,128]{1,0:T(8,128)(2,1)S(1)}, u32[]{:S(2)}, u32[]{:S(2)}) collective-permute-start(bf16[1072,128]{1,0:T(8,128)(2,1)S(1)} %leave_next.1), channel_id=1, source_target_pairs={{0,4},{4,0},{8,12},{12,8},{16,20},{20,16},{24,28},{28,24},{32,36},... | collective-permute-start | bytes 823304 | tf_op jit(solution)/shard_map/ppermute | solution.py:271
  61.0 0.2 leave_own.1
  61.3 0.1 collective-permute-start.10
  61.4 0.9 collective-permute-done.11.other
  62.2 0.4 pass_on.3
  62.6 0.5 collective-permute-start.16
  63.1 0.4 pass_on.2
  63.6 5.2 %collective-permute-done.16.back = bf16[560,128]{1,0:T(8,128)(2,1)S(1)} collective-permute-done((bf16[560,128]{1,0:T(8,128)(2,1)S(1)}, bf16[560,128]{1,0:T(8,128)(2,1)S(1)}, u32[]{:S(2)}, u32[]{:S(2)}) %collective-permute-start.16) | collective-permute-done | bytes 143392 | tf_op jit(solution)/shard_map/ppermute | solution.py:271
  68.9 0.5 join.3.own
  69.4 2.8 %collective-permute-start.19 = (bf16[512,128]{1,0:T(8,128)(2,1)S(1)}, bf16[512,128]{1,0:T(8,128)(2,1)S(1)}, u32[]{:S(2)}, u32[]{:S(2)}) collective-permute-start(bf16[512,128]{1,0:T(8,128)(2,1)S(1)} %join.3.own), channel_id=1, source_target_pairs={{0,2},{1,3},{2,0},{3,1},{4,6},{5,7},{6,4},{7,5},{8,10},{9,11},{10,... | collective-permute-start | bytes 393224 | tf_op jit(solution)/shard_map/ppermute | solution.py:293
  72.3 0.9 collective-permute-start.18
  73.1 0.6 collective-permute-start.17
  73.7 0.5 join.2.own
  74.3 1.1 %collective-permute-start.15 = (bf16[512,128]{1,0:T(8,128)(2,1)S(1)}, bf16[512,128]{1,0:T(8,128)(2,1)S(1)}, u32[]{:S(2)}, u32[]{:S(2)}) collective-permute-start(bf16[512,128]{1,0:T(8,128)(2,1)S(1)} %join.2.own), channel_id=1, source_target_pairs={{0,2},{1,3},{2,0},{3,1},{4,6},{5,7},{6,4},{7,5},{8,10},{9,11},{10,... | collective-permute-start | bytes 393224 | tf_op jit(solution)/shard_map/ppermute | solution.py:293
  75.3 1.7 %collective-permute-start.14 = (bf16[512,128]{1,0:T(8,128)(2,1)S(1)}, bf16[512,128]{1,0:T(8,128)(2,1)S(1)}, u32[]{:S(2)}, u32[]{:S(2)}) collective-permute-start(bf16[512,128]{1,0:T(8,128)(2,1)S(1)} %join.2.own), channel_id=1, source_target_pairs={{0,3},{1,0},{2,1},{3,2},{4,7},{5,4},{6,5},{7,6},{8,11},{9,8},{10,9... | collective-permute-start | bytes 393224 | tf_op jit(solution)/shard_map/ppermute | solution.py:293
  77.1 2.8 %collective-permute-done.17.left = bf16[512,128]{1,0:T(8,128)(2,1)S(1)} collective-permute-done((bf16[512,128]{1,0:T(8,128)(2,1)S(1)}, bf16[512,128]{1,0:T(8,128)(2,1)S(1)}, u32[]{:S(2)}, u32[]{:S(2)}) %collective-permute-start.17) | collective-permute-done | bytes 131104 | tf_op jit(solution)/shard_map/ppermute | solution.py:293
  79.9 2.6 %project.2.refs_0_ = bf16[1024,1536]{1,0:T(8,128)(2,1)} custom-call(s32[1]{0:T(128)} %bitcast.heads, bf16[512,128]{1,0:T(8,128)(2,1)S(1)} %join.3.own, bf16[512,128]{1,0:T(8,128)(2,1)S(1)} %collective-permute-done.17.left, bf16[512,128]{1,0:T(8,128)(2,1)S(1)} %collective-permute-done.18.right, bf16[512,128]{1,0:T(8,128)(2,1)S(1)} %collective-permute-done.19.far, ...), custom_call_target="tpu_custom_call" | custom-call | flops 805306368 | bytes 1572864 | tf_op jit(solution)/shard_map/project/pallas_call | solution.py:238
  82.5 0.4 collective-permute-done.14.right
  82.9 2.2 %collective-permute-done.13.left = bf16[512,128]{1,0:T(8,128)(2,1)S(1)} collective-permute-done((bf16[512,128]{1,0:T(8,128)(2,1)S(1)}, bf16[512,128]{1,0:T(8,128)(2,1)S(1)}, u32[]{:S(2)}, u32[]{:S(2)}) %collective-permute-start.13) | collective-permute-done | bytes 131104 | tf_op jit(solution)/shard_map/ppermute | solution.py:293
  85.1 2.6 %project.3 = bf16[1024,1536]{1,0:T(8,128)(2,1)} custom-call(s32[1]{0:T(128)} %bitcast.heads, bf16[512,128]{1,0:T(8,128)(2,1)S(1)} %join.2.own, bf16[512,128]{1,0:T(8,128)(2,1)S(1)} %collective-permute-done.13.left, bf16[512,128]{1,0:T(8,128)(2,1)S(1)} %collective-permute-done.14.right, ...), custom_call_target="tpu_custom_call", output_to_operand_aliasing={{}: (6, {})} | custom-call | flops 805306368 | bytes 1572864 | tf_op jit(solution)/shard_map/project/pallas_call | solution.py:238
  (21 shorter events, 0.5 us)
Async XLA Ops:
  1.1 16.2 %collective-permute-start.3 = (bf16[2,1024,128]{2,1,0:T(8,128)(2,1)S(1)}, bf16[2,1024,128]{2,1,0:T(8,128)(2,1)S(1)}, u32[]{:S(2)}, u32[]{:S(2)}) collective-permute-start(bf16[2,1024,128]{2,1,0:T(8,128)(2,1)S(1)} %pad_maximum_fusion.refs_1_.refs_2_), channel_id=1, source_target_pairs={{0,8},{4,60},{8,16},{12,4},{16,24},{20,12},{24,32},{28,20},{32,40}... | collective-permute-start | bytes 1572872 | tf_op jit(solution)/shard_map/ppermute | solution.py:271
  8.9 15.8 %collective-permute-start.5 = (bf16[2,1024,128]{2,1,0:T(8,128)(2,1)S(1)}, bf16[2,1024,128]{2,1,0:T(8,128)(2,1)S(1)}, u32[]{:S(2)}, u32[]{:S(2)}) collective-permute-start(bf16[2,1024,128]{2,1,0:T(8,128)(2,1)S(1)} %pad_maximum_fusion.refs_1_.refs_2_), channel_id=1, source_target_pairs={{0,60},{4,8},{8,4},{12,16},{16,12},{20,24},{24,20},{28,32},{32,28}... | collective-permute-start | bytes 1572872 | tf_op jit(solution)/shard_map/ppermute | solution.py:271
  8.9 7.8 %collective-permute-start = (bf16[1024,128]{1,0:T(8,128)(2,1)}, bf16[1024,128]{1,0:T(8,128)(2,1)S(1)}, u32[]{:S(2)}, u32[]{:S(2)}) collective-permute-start(bf16[1024,128]{1,0:T(8,128)(2,1)} %refs_0_.15), channel_id=1, source_target_pairs={{0,4},{4,0},{8,12},{12,8},{16,20},{20,16},{24,28},{28,24},{32,36},... | collective-permute-start | bytes 786440 | tf_op jit(solution)/shard_map/ppermute | solution.py:271
  10.0 9.7 %collective-permute-start.2 = (bf16[1024,128]{1,0:T(8,128)(2,1)}, bf16[1024,128]{1,0:T(8,128)(2,1)S(1)}, u32[]{:S(2)}, u32[]{:S(2)}) collective-permute-start(bf16[1024,128]{1,0:T(8,128)(2,1)} %refs_0_.15), channel_id=1, source_target_pairs={{0,196},{4,192},{8,204},{12,200},{16,212},{20,208},{24,220},{28,21... | collective-permute-start | bytes 786440 | tf_op jit(solution)/shard_map/ppermute | solution.py:271
  12.6 11.4 %collective-permute-start.1 = (bf16[1024,128]{1,0:T(8,128)(2,1)}, bf16[1024,128]{1,0:T(8,128)(2,1)S(1)}, u32[]{:S(2)}, u32[]{:S(2)}) collective-permute-start(bf16[1024,128]{1,0:T(8,128)(2,1)} %refs_0_.15), channel_id=1, source_target_pairs={{0,192},{4,196},{8,200},{12,204},{16,208},{20,212},{24,216},{28,22... | collective-permute-start | bytes 786440 | tf_op jit(solution)/shard_map/ppermute | solution.py:271
  13.1 1.0 %copy-start.1 = (bf16[1024,128]{1,0:T(8,128)(2,1)S(1)}, bf16[1024,128]{1,0:T(8,128)(2,1)}, u32[]{:S(2)}) copy-start(bf16[1024,128]{1,0:T(8,128)(2,1)} %refs_0_.15) | copy-start | bytes 786436
  17.2 9.1 %collective-permute-start.4 = (bf16[2,1024,128]{2,1,0:T(8,128)(2,1)S(1)}, bf16[2,1024,128]{2,1,0:T(8,128)(2,1)S(1)}, u32[]{:S(2)}, u32[]{:S(2)}) collective-permute-start(bf16[2,1024,128]{2,1,0:T(8,128)(2,1)S(1)} %collective-permute-done.3.refs_4_), channel_id=1, source_target_pairs={{0,8},{4,60},{8,16},{12,4},{16,24},{20,12},{24,32},{28,20},{32,40}... | collective-permute-start | bytes 1572872 | tf_op jit(solution)/shard_map/ppermute | solution.py:271
  24.7 8.1 %collective-permute-start.7 = (bf16[2,1024,128]{2,1,0:T(8,128)(2,1)S(1)}, bf16[2,1024,128]{2,1,0:T(8,128)(2,1)S(1)}, u32[]{:S(2)}, u32[]{:S(2)}) collective-permute-start(bf16[2,1024,128]{2,1,0:T(8,128)(2,1)S(1)} %collective-permute-done.5.refs_4_), channel_id=1, source_target_pairs={{0,8},{4,60},{8,16},{12,4},{16,24},{20,12},{24,32},{28,20},{32,40}... | collective-permute-start | bytes 1572872 | tf_op jit(solution)/shard_map/ppermute | solution.py:271
  26.4 12.4 %collective-permute-start.6 = (bf16[2,1024,128]{2,1,0:T(8,128)(2,1)S(1)}, bf16[2,1024,128]{2,1,0:T(8,128)(2,1)S(1)}, u32[]{:S(2)}, u32[]{:S(2)}) collective-permute-start(bf16[2,1024,128]{2,1,0:T(8,128)(2,1)S(1)} %collective-permute-done.4.refs_4_), channel_id=1, source_target_pairs={{0,8},{4,60},{8,16},{12,4},{16,24},{20,12},{24,32},{28,20},{32,40}... | collective-permute-start | bytes 1572872 | tf_op jit(solution)/shard_map/ppermute | solution.py:271
  32.8 11.6 %collective-permute-start.9 = (bf16[2,1024,128]{2,1,0:T(8,128)(2,1)S(1)}, bf16[2,1024,128]{2,1,0:T(8,128)(2,1)S(1)}, u32[]{:S(2)}, u32[]{:S(2)}) collective-permute-start(bf16[2,1024,128]{2,1,0:T(8,128)(2,1)S(1)} %collective-permute-done.7.refs_4_), channel_id=1, source_target_pairs={{0,8},{4,60},{8,16},{12,4},{16,24},{20,12},{24,32},{28,20},{32,40}... | collective-permute-start | bytes 1572872 | tf_op jit(solution)/shard_map/ppermute | solution.py:271
  38.7 11.2 %collective-permute-start.8 = (bf16[2,1024,128]{2,1,0:T(8,128)(2,1)S(1)}, bf16[2,1024,128]{2,1,0:T(8,128)(2,1)S(1)}, u32[]{:S(2)}, u32[]{:S(2)}) collective-permute-start(bf16[2,1024,128]{2,1,0:T(8,128)(2,1)S(1)} %collective-permute-done.6.refs_4_), channel_id=1, source_target_pairs={{0,8},{4,60},{8,16},{12,4},{16,24},{20,12},{24,32},{28,20},{32,40}... | collective-permute-start | bytes 1572872 | tf_op jit(solution)/shard_map/ppermute | solution.py:271
  54.2 8.0 %collective-permute-start.11 = (bf16[1072,128]{1,0:T(8,128)(2,1)S(1)}, bf16[1072,128]{1,0:T(8,128)(2,1)S(1)}, u32[]{:S(2)}, u32[]{:S(2)}) collective-permute-start(bf16[1072,128]{1,0:T(8,128)(2,1)S(1)} %leave_next.1), channel_id=1, source_target_pairs={{0,4},{4,0},{8,12},{12,8},{16,20},{20,16},{24,28},{28,24},{32,36},... | collective-permute-start | bytes 823304 | tf_op jit(solution)/shard_map/ppermute | solution.py:271
  61.3 2.4 %collective-permute-start.10 = (bf16[1072,128]{1,0:T(8,128)(2,1)S(1)}, bf16[1072,128]{1,0:T(8,128)(2,1)S(1)}, u32[]{:S(2)}, u32[]{:S(2)}) collective-permute-start(bf16[1072,128]{1,0:T(8,128)(2,1)S(1)} %leave_own.1), channel_id=1, source_target_pairs={{0,4},{4,0},{8,12},{12,8},{16,20},{20,16},{24,28},{28,24},{32,36},... | collective-permute-start | bytes 823304 | tf_op jit(solution)/shard_map/ppermute | solution.py:271
  62.6 6.3 %collective-permute-start.16 = (bf16[560,128]{1,0:T(8,128)(2,1)S(1)}, bf16[560,128]{1,0:T(8,128)(2,1)S(1)}, u32[]{:S(2)}, u32[]{:S(2)}) collective-permute-start(bf16[560,128]{1,0:T(8,128)(2,1)S(1)} %pass_on.3), channel_id=1, source_target_pairs={{0,64},{4,68},{8,72},{12,76},{16,80},{20,84},{24,88},{28,92},{32,9... | collective-permute-start | bytes 430088 | tf_op jit(solution)/shard_map/ppermute | solution.py:271
  63.5 10.2 %collective-permute-start.12 = (bf16[560,128]{1,0:T(8,128)(2,1)S(1)}, bf16[560,128]{1,0:T(8,128)(2,1)S(1)}, u32[]{:S(2)}, u32[]{:S(2)}) collective-permute-start(bf16[560,128]{1,0:T(8,128)(2,1)S(1)} %pass_on.2), channel_id=1, source_target_pairs={{0,64},{4,68},{8,72},{12,76},{16,80},{20,84},{24,88},{28,92},{32,9... | collective-permute-start | bytes 430088 | tf_op jit(solution)/shard_map/ppermute | solution.py:271
  69.4 10.4 %copy-start = (bf16[512,1536]{1,0:T(8,128)(2,1)S(1)}, bf16[512,1536]{1,0:T(8,128)(2,1)}, u32[]{:S(2)}) copy-start(bf16[512,1536]{1,0:T(8,128)(2,1)} %weight.3) | copy-start | bytes 4718596
  69.4 7.6 %collective-permute-start.19 = (bf16[512,128]{1,0:T(8,128)(2,1)S(1)}, bf16[512,128]{1,0:T(8,128)(2,1)S(1)}, u32[]{:S(2)}, u32[]{:S(2)}) collective-permute-start(bf16[512,128]{1,0:T(8,128)(2,1)S(1)} %join.3.own), channel_id=1, source_target_pairs={{0,2},{1,3},{2,0},{3,1},{4,6},{5,7},{6,4},{7,5},{8,10},{9,11},{10,... | collective-permute-start | bytes 393224 | tf_op jit(solution)/shard_map/ppermute | solution.py:293
  72.3 4.8 %collective-permute-start.18 = (bf16[512,128]{1,0:T(8,128)(2,1)S(1)}, bf16[512,128]{1,0:T(8,128)(2,1)S(1)}, u32[]{:S(2)}, u32[]{:S(2)}) collective-permute-start(bf16[512,128]{1,0:T(8,128)(2,1)S(1)} %join.3.own), channel_id=1, source_target_pairs={{0,3},{1,0},{2,1},{3,2},{4,7},{5,4},{6,5},{7,6},{8,11},{9,8},{10,9... | collective-permute-start | bytes 393224 | tf_op jit(solution)/shard_map/ppermute | solution.py:293
  73.1 6.7 %collective-permute-start.17 = (bf16[512,128]{1,0:T(8,128)(2,1)S(1)}, bf16[512,128]{1,0:T(8,128)(2,1)S(1)}, u32[]{:S(2)}, u32[]{:S(2)}) collective-permute-start(bf16[512,128]{1,0:T(8,128)(2,1)S(1)} %join.3.own), channel_id=1, source_target_pairs={{0,1},{1,2},{2,3},{3,0},{4,5},{5,6},{6,7},{7,4},{8,9},{9,10},{10,1... | collective-permute-start | bytes 393224 | tf_op jit(solution)/shard_map/ppermute | solution.py:293
  74.3 8.2 %collective-permute-start.15 = (bf16[512,128]{1,0:T(8,128)(2,1)S(1)}, bf16[512,128]{1,0:T(8,128)(2,1)S(1)}, u32[]{:S(2)}, u32[]{:S(2)}) collective-permute-start(bf16[512,128]{1,0:T(8,128)(2,1)S(1)} %join.2.own), channel_id=1, source_target_pairs={{0,2},{1,3},{2,0},{3,1},{4,6},{5,7},{6,4},{7,5},{8,10},{9,11},{10,... | collective-permute-start | bytes 393224 | tf_op jit(solution)/shard_map/ppermute | solution.py:293
  75.3 7.5 %collective-permute-start.14 = (bf16[512,128]{1,0:T(8,128)(2,1)S(1)}, bf16[512,128]{1,0:T(8,128)(2,1)S(1)}, u32[]{:S(2)}, u32[]{:S(2)}) collective-permute-start(bf16[512,128]{1,0:T(8,128)(2,1)S(1)} %join.2.own), channel_id=1, source_target_pairs={{0,3},{1,0},{2,1},{3,2},{4,7},{5,4},{6,5},{7,6},{8,11},{9,8},{10,9... | collective-permute-start | bytes 393224 | tf_op jit(solution)/shard_map/ppermute | solution.py:293
  77.1 8.1 %collective-permute-start.13 = (bf16[512,128]{1,0:T(8,128)(2,1)S(1)}, bf16[512,128]{1,0:T(8,128)(2,1)S(1)}, u32[]{:S(2)}, u32[]{:S(2)}) collective-permute-start(bf16[512,128]{1,0:T(8,128)(2,1)S(1)} %join.2.own), channel_id=1, source_target_pairs={{0,1},{1,2},{2,3},{3,0},{4,5},{5,6},{6,7},{7,4},{8,9},{9,10},{10,1... | collective-permute-start | bytes 393224 | tf_op jit(solution)/shard_map/ppermute | solution.py:293
